TPU v7x, 512 devices: a whole 4x4x16 slice. The times are simulated.
512 devices in a mesh: pool: 32 (over x, z_hi, y), tp: 16 (over z_lo, core).
Axes of the slice: x: 4, y: 4, z: 16 (z_hi: 2, z_lo: 8; z = z_hi * 8 + z_lo), core: 2. Of those that a mesh axis runs over, the one named last changes fastest.
Arguments:
- tokens: bfloat16 [6144, 8192], P('pool', 'tp'), may hold values from -6 to 6
- norm_gain: float32 [8192], replicated, may hold values from 0.1 to 1.9
- doc_lengths: int32 [32, 4], P('pool'), may hold values from 1 to 96, 192 in all within a row
- query_master: float32 [8192, 4096], P('pool', 'tp')
- query_grad: bfloat16 [8192, 4096], P('pool', 'tp'), may hold values from -12 to 12
- query_first: float32 [8192, 4096], P('pool', 'tp'), may hold values from -6 to 6
- query_second: float32 [8192, 4096], P('pool', 'tp'), may hold values from 0.1 to 4
- kv_master: float32 [2, 8192, 512], P(None, 'pool', 'tp')
- kv_grad: bfloat16 [2, 8192, 512], P(None, 'pool', 'tp'), may hold values from -12 to 12
- kv_first: float32 [2, 8192, 512], P(None, 'pool', 'tp'), may hold values from -6 to 6
- kv_second: float32 [2, 8192, 512], P(None, 'pool', 'tp'), may hold values from 0.1 to 4
- out_master: float32 [4096, 8192], P(('tp', 'pool')), may hold values from -0.09375 to 0.09375
- out_grad: bfloat16 [4096, 8192], P(('tp', 'pool')), may hold values from -12 to 12
- out_first: float32 [4096, 8192], P(('tp', 'pool')), may hold values from -6 to 6
- out_second: float32 [4096, 8192], P(('tp', 'pool')), may hold values from 0.1 to 4
Outputs:
- mixed: bfloat16 [6144, 8192], P('pool', 'tp')
- query_master_new: float32 [8192, 4096], P('pool', 'tp')
- query_first_new: float32 [8192, 4096], P('pool', 'tp')
- query_second_new: float32 [8192, 4096], P('pool', 'tp')
- kv_master_new: float32 [2, 8192, 512], P(None, 'pool', 'tp')
- kv_first_new: float32 [2, 8192, 512], P(None, 'pool', 'tp')
- kv_second_new: float32 [2, 8192, 512], P(None, 'pool', 'tp')
- out_master_new: float32 [4096, 8192], P(('tp', 'pool'))
- out_first_new: float32 [4096, 8192], P(('tp', 'pool'))
- out_second_new: float32 [4096, 8192], P(('tp', 'pool'))
Inputs may be any that keep to these rules, and one draw needn't show every extreme that they name: `doc_lengths`: each row holds the lengths of the 4 rollouts of one group and sums to 192; the longest rollout of each row has exactly 96 tokens.
All inputs are finite; a program needn't handle non-finite values.
Results may differ from a plain program's by a relative error of at most 0.023.
Values may be sent and summed in bfloat16 or wider, within the bound.
No kernel may reach another device: no remote copies, remote signals or barrier semaphores. Data moves between devices by JAX's collectives and lax.ppermute only.
A program may use at most 64 MiB of HBM per device.

v0:
```python
import jax
import jax.numpy as jnp
from jax import lax
from jax.sharding import PartitionSpec as P

HEAD_DIM = 128


beta_first = 0.9
beta_second = 0.95
learn_rate = 0.001
adam_eps = 1e-08
norm_eps = 1e-06


def adam_step(master, gradient, first, second):
    grad_value = gradient.astype(jnp.float32)
    first = beta_first * first + (1.0 - beta_first) * grad_value
    second = beta_second * second + (1.0 - beta_second) * grad_value * grad_value
    correct_first = 1.0 - beta_first**10
    correct_second = 1.0 - beta_second**10
    master = master - learn_rate * (first / correct_first) / (
        jnp.sqrt(second / correct_second) + adam_eps
    )
    return (master, first, second, master.astype(jnp.bfloat16))


def shards(
    tokens,
    norm_gain,
    doc_lengths,
    query_master,
    query_grad,
    query_first,
    query_second,
    kv_master,
    kv_grad,
    kv_first,
    kv_second,
    out_master,
    out_grad,
    out_first,
    out_second,
):
    q_master, q_first, q_second, q_weight = adam_step(
        query_master, query_grad, query_first, query_second
    )
    k_master, k_first, k_second, k_weight = adam_step(kv_master, kv_grad, kv_first, kv_second)
    o_master, o_first, o_second, o_weight = adam_step(out_master, out_grad, out_first, out_second)
    whole = lax.all_gather(tokens, "tp", axis=1, tiled=True)
    values_in = whole.astype(jnp.float32)
    scale = lax.rsqrt(jnp.mean(values_in * values_in, axis=-1, keepdims=True) + norm_eps)
    normed = (values_in * scale * norm_gain).astype(jnp.bfloat16)
    row_count = normed.shape[0]

    def add_rows(piece):
        return jnp.einsum("tr,erc->etc", normed, piece, preferred_element_type=jnp.float32)

    query_input = q_weight[None]
    query_proj = add_rows(lax.all_gather(query_input, "pool", axis=1, tiled=True))
    kv_proj = add_rows(lax.all_gather(k_weight, "pool", axis=1, tiled=True))
    query = query_proj[0].astype(jnp.bfloat16)
    kv_all = lax.all_gather(kv_proj.astype(jnp.bfloat16), "tp", axis=2, tiled=True)
    heads_here = query.shape[1] // HEAD_DIM
    kv_count = kv_all.shape[2] // HEAD_DIM
    kv_split = kv_all.reshape(2, row_count, kv_count, HEAD_DIM)
    head_ids = (
        lax.axis_index("tp") * heads_here + jnp.arange(heads_here, dtype=jnp.int32)
    ) % kv_count
    kv_pick = jnp.take(kv_split, head_ids, axis=2)
    keys = kv_pick[0]
    values = kv_pick[1]
    ends = jnp.cumsum(doc_lengths[0])
    positions = jnp.arange(row_count, dtype=jnp.int32)
    segment = jnp.sum((ends[None, :] <= positions[:, None]).astype(jnp.int32), axis=1)
    allowed = (segment[:, None] == segment[None, :]) & (positions[None, :] <= positions[:, None])
    query_heads = query.reshape(row_count, heads_here, HEAD_DIM)
    scores = jnp.einsum(
        "thd,shd->hts", query_heads, keys, preferred_element_type=jnp.float32
    ) * HEAD_DIM ** (-0.5)
    scores = jnp.where(allowed[None], scores, -1e30)
    scores = scores - jnp.max(scores, axis=-1, keepdims=True)
    weights = jnp.exp(scores)
    weights = (weights / jnp.sum(weights, axis=-1, keepdims=True)).astype(jnp.bfloat16)
    context = jnp.einsum("hts,shd->thd", weights, values, preferred_element_type=jnp.float32)
    context = context.astype(jnp.bfloat16).reshape(row_count, heads_here * HEAD_DIM)
    terms = jnp.dot(
        context,
        lax.all_gather(o_weight, "pool", axis=0, tiled=True),
        preferred_element_type=jnp.float32,
    )
    mixed = lax.psum_scatter(terms.astype(jnp.bfloat16), "tp", scatter_dimension=1, tiled=True)
    return (
        mixed,
        q_master,
        q_first,
        q_second,
        k_master,
        k_first,
        k_second,
        o_master,
        o_first,
        o_second,
    )


def solution(mesh):
    in_specs = (
        P("pool", "tp"),
        P(),
        P("pool", None),
        P("pool", "tp"),
        P("pool", "tp"),
        P("pool", "tp"),
        P("pool", "tp"),
        P(None, "pool", "tp"),
        P(None, "pool", "tp"),
        P(None, "pool", "tp"),
        P(None, "pool", "tp"),
        P(("tp", "pool"), None),
        P(("tp", "pool"), None),
        P(("tp", "pool"), None),
        P(("tp", "pool"), None),
    )
    out_specs = (
        P("pool", "tp"),
        P("pool", "tp"),
        P("pool", "tp"),
        P("pool", "tp"),
        P(None, "pool", "tp"),
        P(None, "pool", "tp"),
        P(None, "pool", "tp"),
        P(("tp", "pool"), None),
        P(("tp", "pool"), None),
        P(("tp", "pool"), None),
    )
    return jax.shard_map(shards, mesh=mesh, in_specs=in_specs, out_specs=out_specs, check_vma=False)
```

profile of v0, /device:TPU:1, one launch (start us, length us, event | category | flops | bytes accessed | tf_op | source)
XLA Modules:
  0.0 678.9 jit_solution(14924305765057743245)
XLA Ops:
  7.2 0.7 all-gather.8.cloned.1.call-update
  8.0 1.6 fusion.51
  9.6 0.0 all-gather.12.cloned.1.call-start
  9.7 2.2 fusion.48
  11.9 2.2 fusion.54
  14.2 0.0 reduce-scatter.2.cloned.1.call-start
  14.2 0.2 reduce-window.8
  14.5 0.1 convert_reduce_fusion
  14.5 0.7 fusion.24
  15.3 102.6 %all-gather.8.cloned.1.call-done = bf16[192,8192]{1,0:T(8,128)(2,1)} async-done(((bf16[192,512]{1,0:T(8,128)(2,1)}), bf16[192,8192]{1,0:T(8,128)(2,1)}) %all-gather.8.cloned.1.call-update) | async-done | bytes 3145744 | tf_op jit(solution)/shard_map/all_gather | solution.py:50
  117.9 2.6 fusion.1
  120.5 119.0 %all-gather.6.cloned.1.call-done = bf16[2,8192,32]{1,2,0:T(8,128)(2,1)} async-done(((bf16[2,256,32]{1,2,0:T(8,128)(2,1)}), bf16[2,8192,32]{1,2,0:T(8,128)(2,1)}) %all-gather.6.cloned.1.call-update) | async-done | bytes 1048592 | tf_op jit(solution)/shard_map/all_gather | solution.py:61
  239.5 3.4 fusion.14
  242.9 31.5 %all_gather.17 = bf16[2,192,512]{1,2,0:T(8,128)(2,1)} all-gather(bf16[2,192,32]{1,2,0:T(8,128)(2,1)S(1)} %fusion.14), channel_id=1, replica_groups=mesh['pool'=32,'tp'=16] {'tp'}, dimensions={2}, use_global_device_ids=true | all-gather | bytes 417792 | tf_op jit(solution)/shard_map/all_gather | solution.py:63
  274.4 1.3 copy.32
  275.7 1.2 gather_fusion
  276.9 1.0 fusion.23
  278.0 117.6 %all-gather.12.cloned.1.call-done = bf16[8192,256]{1,0:T(8,128)(2,1)} async-done(((bf16[256,256]{1,0:T(8,128)(2,1)}), bf16[8192,256]{1,0:T(8,128)(2,1)}) %all-gather.12.cloned.1.call-update) | async-done | bytes 4194320 | tf_op jit(solution)/shard_map/all_gather | solution.py:60
  395.5 3.2 fusion.10
  398.8 0.3 fusion.57
  399.1 0.5 fusion.9
  399.6 161.6 %all-gather.10.cloned.1.call-done = bf16[256,8192]{1,0:T(8,128)(2,1)} async-done(((bf16[8,8192]{1,0:T(8,128)(2,1)}), bf16[256,8192]{1,0:T(8,128)(2,1)}) %all-gather.10.cloned.1.call-update) | async-done | bytes 4194320 | tf_op jit(solution)/shard_map/all_gather | solution.py:89
  561.3 4.9 convolution_convert_fusion
  566.2 106.2 %reduce-scatter.2.cloned.1.call-done = bf16[192,512]{1,0:T(8,128)(2,1)} async-done(((bf16[192,8192]{1,0:T(8,128)(2,1)}), bf16[192,512]{1,0:T(8,128)(2,1)}) %reduce-scatter.2.cloned.1.call-update) | async-done | bytes 196624 | tf_op jit(solution)/shard_map/reduce_scatter | solution.py:92
  (20 shorter events, 0.3 us)
Async XLA Ops:
  7.2 7.0 %copy-start.3 = (s32[1,4]{1,0:T(1,128)S(1)}, s32[1,4]{1,0:T(1,128)}, u32[]{:S(2)}) copy-start(s32[1,4]{1,0:T(1,128)} %param.17) | copy-start | bytes 52
  7.2 232.3 %copy-start.2 = (f32[8192]{0:T(1024)S(1)}, f32[8192]{0:T(1024)}, u32[]{:S(2)}) copy-start(f32[8192]{0:T(1024)} %param.16) | copy-start | bytes 98308
  7.2 110.7 %all-gather.8.cloned.1.call-start = ((), (), s32[]{:S(2)}) async-start(), calls=%async_computation.2 | async-start | bytes 3342336 | tf_op jit(solution)/shard_map/all_gather | solution.py:50
  7.9 231.6 %all-gather.6.cloned.1.call-start = ((), (), s32[]{:S(2)}) async-start(), calls=%async_computation.1 | async-start | bytes 1081344 | tf_op jit(solution)/shard_map/all_gather | solution.py:61
  9.6 385.9 %all-gather.12.cloned.1.call-start = ((), (), s32[]{:S(2)}) async-start(), calls=%async_computation.5 | async-start | bytes 4325376 | tf_op jit(solution)/shard_map/all_gather | solution.py:60
  11.9 549.4 %all-gather.10.cloned.1.call-start = ((), (), s32[]{:S(2)}) async-start(), calls=%async_computation.3 | async-start | bytes 4325376 | tf_op jit(solution)/shard_map/all_gather | solution.py:89
  14.2 658.2 %reduce-scatter.2.cloned.1.call-start = ((), (), s32[]{:S(2)}) async-start(), calls=%async_computation.4 | async-start | bytes 3342336 | tf_op jit(solution)/shard_map/reduce_scatter | solution.py:92
  120.5 275.1 %copy-start = (bf16[192,8192]{1,0:T(8,128)(2,1)S(1)}, bf16[192,8192]{1,0:T(8,128)(2,1)}, u32[]{:S(2)}) copy-start(bf16[192,8192]{1,0:T(8,128)(2,1)} %all-gather.8.cloned.1.call-done) | copy-start | bytes 9437188
  278.0 120.9 %copy-start.1 = (pred[192,192]{0,1:T(8,128)(4,1)S(1)}, pred[192,192]{0,1:T(8,128)(4,1)}, u32[]{:S(2)}) copy-start(pred[192,192]{0,1:T(8,128)(4,1)} %fusion.24) | copy-start | bytes 110596
Sparse Core Ops, SparseCore 0:
  10.1 107.6 all-gather.7
  122.5 116.9 all-gather.5
  243.9 151.5 all-gather.11
  399.8 161.4 all-gather.9
  566.3 106.0 reduce-scatter.1
where the time goes:
time: 686 us; the launch traced here: 679 us
  waiting for transfers between devices  608 us (89%)
  blocking collectives  31.5 us (5%)
  between operations  13.9 us (2%)
  matrix products  12.3 us (2%)
  other arithmetic  10.7 us (2%)
    all_gather x1, waiting for transfers between devices, shards(): lax.all_gather(o_weight, 'pool', axis=0, tiled=True)  162 us
    all_gather x1, waiting for transfers between devices, shards(): kv_proj = add_rows(lax.all_gather(k_weight, 'pool', axis=1, tiled=True))  119 us
    all_gather x1, waiting for transfers between devices, shards(): lax.all_gather(query_input, 'pool', axis=1, tiled=True)  118 us
    reduce_scatter x1, waiting for transfers between devices, shards(): lax.psum_scatter(terms.astype(jnp.bfloat16), 'tp', scatter_dimension=1, t...  106 us
    all_gather x1, waiting for transfers between devices, shards(): whole = lax.all_gather(tokens, 'tp', axis=1, tiled=True)  103 us
    all_gather x1, blocking collectives, shards(): lax.all_gather(kv_proj.astype(jnp.bfloat16), 'tp', axis=2, tiled=True)  31.5 us
  transfers between devices with their start and end apart: 5, of which 5 were waited for; matrix products, arithmetic and copies ran while one was open for 3% of the time, Pallas kernels for 0%

commit v1 on v0

v1 whole, which is shorter than its diff:
```python
import jax
import jax.numpy as jnp
from jax import lax
from jax.experimental import pallas as pl
from jax.experimental.pallas import tpu as pltpu
from jax.sharding import Mesh, PartitionSpec as P

HEAD_DIM = 128
ROWS = 192
MIB = 1 << 20

beta_first = 0.9
beta_second = 0.95
learn_rate = 0.001
adam_eps = 1e-08
norm_eps = 1e-06

STEPS = (4, 2, 1)
ORDER = (0, 4, 2, 6, 1, 5, 3, 7)


def adam_step(master, gradient, first, second):
    grad_value = gradient.astype(jnp.float32)
    first = beta_first * first + (1.0 - beta_first) * grad_value
    second = beta_second * second + (1.0 - beta_second) * grad_value * grad_value
    correct_first = 1.0 - beta_first**10
    correct_second = 1.0 - beta_second**10
    master = master - learn_rate * (first / correct_first) / (
        jnp.sqrt(second / correct_second) + adam_eps
    )
    return (master, first, second, master.astype(jnp.bfloat16))


def swap_z(value, bit):
    return lax.ppermute(value, "z", [(z, z ^ bit) for z in range(8)])


def swap_core(value):
    return lax.ppermute(value, "c", [(0, 1), (1, 0)])


def swap_half(value):
    return lax.ppermute(value, "h", [(0, 1), (1, 0)])


def gather_plane(value):
    whole = jnp.broadcast_to(value[None], (16,) + value.shape)
    return lax.all_to_all(whole, ("x", "y"), 0, 0, tiled=True)


def vmem(count):
    return [pl.BlockSpec(memory_space=pltpu.VMEM)] * count


def smem():
    return pl.BlockSpec(memory_space=pltpu.SMEM)


def params(mib):
    return pltpu.CompilerParams(vmem_limit_bytes=mib * MIB)


def norm_kernel(place, gain, near, far, core_near, core_far, out):
    z, c = place[0], place[1]
    blocks = []
    for other, pair in enumerate(((near, far), (core_near, core_far))):
        for at in range(8):
            blocks.append((other, at, pair[at // 4], at % 4))

    def chunk(i, carry):
        rows = pl.ds(pl.multiple_of(i * 16, 16), 16)
        total = jnp.zeros((16, 512), jnp.float32)
        for _, _, ref, at in blocks:
            value = ref[at, rows, :].astype(jnp.float32)
            total = total + value * value
        mean = jnp.sum(total, axis=-1, keepdims=True) * (1.0 / 8192)
        scale = lax.rsqrt(mean + norm_eps)
        for other, place_at, ref, at in blocks:
            value = ref[at, rows, :].astype(jnp.float32)
            features = (z ^ ORDER[place_at]) * 2 + (c ^ other)
            value = value * scale * gain[features]
            out[other, place_at, rows, :] = value.astype(jnp.bfloat16)
        return carry

    lax.fori_loop(0, ROWS // 16, chunk, 0)


def norm_tokens(place, gain, near, far, core_near, core_far):
    return pl.pallas_call(
        norm_kernel,
        out_shape=jax.ShapeDtypeStruct((2, 8, ROWS, 512), jnp.bfloat16),
        in_specs=[smem()] + vmem(5),
        out_specs=vmem(1)[0],
        compiler_params=params(24),
        cost_estimate=pl.CostEstimate(
            flops=8 * ROWS * 8192, bytes_accessed=6 * MIB, transcendentals=0
        ),
        name="norm_tokens",
    )(place, gain, near, far, core_near, core_far)


def feature_block(place, normed, x, y, slot):
    z, c, h = place[0], place[1], place[2]
    z_rel = (x * 2 + (slot ^ h)) ^ z
    at = ((z_rel & 1) * 4) | (z_rel & 2) | (z_rel // 4)
    return normed[(y // 2) ^ c, at, :, (y % 2) * 256 : (y % 2) * 256 + 256]


def kv_kernel(place, normed, weight, out):
    total = jnp.zeros((64, ROWS), jnp.float32)
    for x in range(4):
        for y in range(4):
            for slot in range(2):
                total = total + lax.dot_general(
                    weight[x * 4 + y, slot],
                    feature_block(place, normed, x, y, slot),
                    (((1,), (1,)), ((), ())),
                    preferred_element_type=jnp.float32,
                )
    out[...] = total.astype(jnp.bfloat16)


def project_kv(place, normed, weight):
    return pl.pallas_call(
        kv_kernel,
        out_shape=jax.ShapeDtypeStruct((64, ROWS), jnp.bfloat16),
        in_specs=[smem()] + vmem(2),
        out_specs=vmem(1)[0],
        compiler_params=params(16),
        cost_estimate=pl.CostEstimate(
            flops=2 * ROWS * 8192 * 64, bytes_accessed=4 * MIB, transcendentals=0
        ),
        name="project_kv",
    )(place, normed, weight)


def query_kernel(place, normed, weight, out, total):
    step = pl.program_id(0)

    @pl.when(step == 0)
    def _():
        total[...] = jnp.zeros_like(total)

    part = jnp.zeros((ROWS, 256), jnp.float32)
    for y in range(4):
        for slot in range(2):
            part = part + jnp.dot(
                feature_block(place, normed, step, y, slot),
                weight[y, slot],
                preferred_element_type=jnp.float32,
            )
    total[...] += part

    @pl.when(step == 3)
    def _():
        out[...] = total[...].astype(jnp.bfloat16)


def project_query(place, normed, weight):
    return pl.pallas_call(
        query_kernel,
        grid=(4,),
        out_shape=jax.ShapeDtypeStruct((ROWS, 256), jnp.bfloat16),
        in_specs=[
            smem(),
            pl.BlockSpec((2, 8, ROWS, 512), lambda i: (0, 0, 0, 0)),
            pl.BlockSpec((4, 2, 256, 256), lambda i: (i, 0, 0, 0)),
        ],
        out_specs=pl.BlockSpec((ROWS, 256), lambda i: (0, 0)),
        scratch_shapes=[pltpu.VMEM((ROWS, 256), jnp.float32)],
        compiler_params=params(24),
        cost_estimate=pl.CostEstimate(
            flops=2 * ROWS * 8192 * 256, bytes_accessed=7 * MIB, transcendentals=0
        ),
        name="project_query",
    )(place, normed, weight)


def attend_kernel(place, lengths, query, pieces, out, held):
    z = place[0]
    for at in range(8):
        held[z ^ ORDER[at]] = pieces[at]
    query_at = lax.broadcasted_iota(jnp.int32, (ROWS, ROWS), 0)
    key_at = lax.broadcasted_iota(jnp.int32, (ROWS, ROWS), 1)
    query_doc = jnp.zeros((ROWS, ROWS), jnp.int32)
    key_doc = jnp.zeros((ROWS, ROWS), jnp.int32)
    end = 0
    for doc in range(4):
        end = end + lengths[0, doc]
        query_doc = query_doc + (query_at >= end).astype(jnp.int32)
        key_doc = key_doc + (key_at >= end).astype(jnp.int32)
    allowed = (query_doc == key_doc) & (key_at <= query_at)
    for head in range(2):
        keys = held[head * 4 : head * 4 + 4, 0:32, :].reshape(HEAD_DIM, ROWS)
        values = held[head * 4 : head * 4 + 4, 32:64, :].reshape(HEAD_DIM, ROWS)
        columns = slice(head * HEAD_DIM, (head + 1) * HEAD_DIM)
        scores = jnp.dot(query[:, columns], keys, preferred_element_type=jnp.float32)
        scores = jnp.where(allowed, scores * HEAD_DIM**-0.5, -1e30)
        scores = scores - jnp.max(scores, axis=-1, keepdims=True)
        weights = jnp.exp(scores)
        weights = weights / jnp.sum(weights, axis=-1, keepdims=True)
        context = lax.dot_general(
            weights.astype(jnp.bfloat16),
            values,
            (((1,), (1,)), ((), ())),
            preferred_element_type=jnp.float32,
        )
        out[:, columns] = context.astype(jnp.bfloat16)


def attend(place, lengths, query, pieces):
    return pl.pallas_call(
        attend_kernel,
        out_shape=jax.ShapeDtypeStruct((ROWS, 256), jnp.bfloat16),
        in_specs=[smem(), smem()] + vmem(2),
        out_specs=vmem(1)[0],
        scratch_shapes=[pltpu.VMEM((8, 64, ROWS), jnp.bfloat16)],
        compiler_params=params(16),
        cost_estimate=pl.CostEstimate(
            flops=8 * ROWS * ROWS * HEAD_DIM,
            bytes_accessed=MIB // 2,
            transcendentals=2 * ROWS * ROWS,
        ),
        name="attend",
    )(place, lengths, query, pieces)


def output_kernel(place, near, far, weight, out, *, other):
    z, c = place[0], place[1]
    start = pl.multiple_of((c ^ other) * 512, 512)
    total = jnp.zeros((ROWS, 512), jnp.float32)
    for at in range(8):
        part = (near if at < 4 else far)[at % 4]
        total = total + jnp.dot(
            part,
            weight[z ^ ORDER[at], :, pl.ds(start, 512)],
            preferred_element_type=jnp.float32,
        )
    out[...] = total.astype(out.dtype)


def project_output(place, near, far, weight, other):
    def kernel(*refs):
        output_kernel(*refs, other=other)

    return pl.pallas_call(
        kernel,
        out_shape=jax.ShapeDtypeStruct(
            (ROWS, 512), jnp.bfloat16 if other else jnp.float32
        ),
        in_specs=[smem()] + vmem(3),
        out_specs=vmem(1)[0],
        compiler_params=params(24),
        cost_estimate=pl.CostEstimate(
            flops=2 * ROWS * 2048 * 512, bytes_accessed=5 * MIB, transcendentals=0
        ),
        name="output_other" if other else "output_own",
    )(place, near, far, weight)


def rotate(index):
    return ((index * 2) & 15) | (index // 8)


def shards(
    tokens,
    norm_gain,
    doc_lengths,
    query_master,
    query_grad,
    query_first,
    query_second,
    kv_master,
    kv_grad,
    kv_first,
    kv_second,
    out_master,
    out_grad,
    out_first,
    out_second,
):
    h = lax.axis_index("h")
    place = jnp.stack([lax.axis_index("z"), lax.axis_index("c"), h]).astype(jnp.int32)

    with jax.named_scope("tokens"):
        near = tokens[None]
        for bit in STEPS[:2]:
            near = jnp.concatenate([near, swap_z(near, bit)])
        far = swap_z(near, STEPS[2])
        core_near = swap_core(near)
        core_far = swap_core(far)

    with jax.named_scope("adam"):
        q_master, q_first, q_second, q_weight = adam_step(
            query_master, query_grad, query_first, query_second
        )
        k_master, k_first, k_second, k_weight = adam_step(
            kv_master, kv_grad, kv_first, kv_second
        )
        o_master, o_first, o_second, o_weight = adam_step(
            out_master, out_grad, out_first, out_second
        )

    with jax.named_scope("kv_weight"):
        k_rows = k_weight.transpose(0, 2, 1).reshape(64, 256)
        own = lax.ppermute(k_rows, ("z", "c"), [(i, rotate(i)) for i in range(16)])
        crossed = lax.ppermute(
            k_rows,
            ("h", "z", "c"),
            [(i * 16 + j, (1 - i) * 16 + rotate(j)) for i in range(2) for j in range(16)],
        )
        kv_whole = gather_plane(jnp.stack([own, crossed]))

    with jax.named_scope("query_weight"):
        q_whole = gather_plane(jnp.stack([q_weight, swap_half(q_weight)]))

    with jax.named_scope("out_weight"):
        o_parts = o_weight.reshape(8, 8, 1024).transpose(1, 0, 2)
        o_parts = lax.all_to_all(o_parts, "z", 0, 0, tiled=True)
        o_crossed = swap_half(o_parts)
        o_halves = jnp.where(
            h == 0, jnp.stack([o_parts, o_crossed]), jnp.stack([o_crossed, o_parts])
        )
        o_whole = lax.all_gather(o_halves, ("x", "y"), axis=0, tiled=False)
        o_whole = o_whole.reshape(4, 4, 2, 8, 8, 1024).transpose(3, 0, 2, 1, 4, 5)
        o_whole = o_whole.reshape(8, 256, 1024)

    with jax.named_scope("projections"):
        gain = norm_gain.reshape(16, 1, 512)
        normed = norm_tokens(place, gain, near, far, core_near, core_far)
        pieces = project_kv(place, normed, kv_whole)[None]
        for bit in STEPS:
            pieces = jnp.concatenate([pieces, swap_z(pieces, bit)])
        query = project_query(place, normed, q_whole)

    with jax.named_scope("attention"):
        context = attend(place, doc_lengths, query, pieces)[None]
        for bit in STEPS[:2]:
            context = jnp.concatenate([context, swap_z(context, bit)])
        context_far = swap_z(context, STEPS[2])

    with jax.named_scope("output"):
        sent = swap_core(project_output(place, context, context_far, o_whole, 1))
        kept = project_output(place, context, context_far, o_whole, 0)
        mixed = (kept + sent.astype(jnp.float32)).astype(jnp.bfloat16)

    return (
        mixed,
        q_master,
        q_first,
        q_second,
        k_master,
        k_first,
        k_second,
        o_master,
        o_first,
        o_second,
    )


def solution(mesh):
    pool, tp = ("x", "h", "y"), ("z", "c")
    split = Mesh(mesh.devices.reshape(4, 2, 4, 8, 2), ("x", "h", "y", "z", "c"))
    weight = P(pool, tp)
    kv_weight = P(None, pool, tp)
    out_weight = P(tp + pool, None)
    in_specs = (
        (P(pool, tp), P(), P(pool, None))
        + (weight,) * 4
        + (kv_weight,) * 4
        + (out_weight,) * 4
    )
    out_specs = (P(pool, tp),) + (weight,) * 3 + (kv_weight,) * 3 + (out_weight,) * 3
    return jax.shard_map(
        shards, mesh=split, in_specs=in_specs, out_specs=out_specs, check_vma=False
    )
```

time: 686 us -> 266 us (0.39)
  waiting for transfers between devices: 608 us -> 124 us
  starting transfers between devices: 0.2 us -> 70 us
  local copies, waits for them, and re-layouts: 2.6 us -> 15.6 us
  matrix products: 12.3 us -> 0 us
  Pallas kernels: 0 us -> 11.4 us
  blocking collectives: 31.5 us -> 23.2 us
    all_gather x4 -> x1, waiting for transfers between devices: 501 us -> 0.02 us  [shards(): o_whole = lax.all_gather(o_halves, ('x', 'y'), axis=0, tiled=False)]
    ppermute x0 -> x16, waiting for transfers between devices: none -> 124 us  [the longest x9 93.1 us: swap_z(): return lax.ppermute(value, 'z', [(z, z ^ bit) for z in range(8)])]
    reduce_scatter x1 -> x0, waiting for transfers between devices: 106 us -> none  [shards(): lax.psum_scatter(terms.astype(jnp.bfloat16), 'tp', scatter_dimension=1, t...]
    ppermute x0 -> x16, starting transfers between devices: none -> 56.3 us  [the longest x9 19.7 us: swap_z(): return lax.ppermute(value, 'z', [(z, z ^ bit) for z in range(8)])]
    all_gather x1 -> x0, blocking collectives: 31.5 us -> none  [shards(): lax.all_gather(kv_proj.astype(jnp.bfloat16), 'tp', axis=2, tiled=True)]
    all_to_all x0 -> x1, blocking collectives: none -> 23.2 us  [shards(): o_parts = lax.all_to_all(o_parts, 'z', 0, 0, tiled=True)]
    all_to_all x0 -> x2, starting transfers between devices: none -> 13.6 us  [gather_plane(): return lax.all_to_all(whole, ('x', 'y'), 0, 0, tiled=True)]
    dot_general x4 -> x0, matrix products: 12 us -> none  [the longest x2 6.63 us: add_rows(): jnp.einsum('tr,erc->etc', normed, piece, preferred_element_type=jnp.float32)]
  transfers between devices with their start and end apart: 5 -> 19, of which waited for: 5 -> 12; matrix products, arithmetic and copies ran while one was open for 3% -> 3% of each run, Pallas kernels for 0% -> 4%
where the time goes in v1:
time: 266 us; the launch traced here: 265 us
  waiting for transfers between devices  124 us (47%)
  starting transfers between devices  70 us (26%)
  blocking collectives  23.2 us (9%)
  local copies, waits for them, and re-layouts  15.6 us (6%)
  between operations  14.4 us (5%)
  Pallas kernels  11.4 us (4%)
  other arithmetic  6.64 us (2%)
    ppermute x9, waiting for transfers between devices, swap_z(): return lax.ppermute(value, 'z', [(z, z ^ bit) for z in range(8)])  93.1 us
    ppermute x2, waiting for transfers between devices, swap_half(): return lax.ppermute(value, 'h', [(0, 1), (1, 0)])  24.4 us
    all_to_all x1, blocking collectives, shards(): o_parts = lax.all_to_all(o_parts, 'z', 0, 0, tiled=True)  23.2 us
    ppermute x9, starting transfers between devices, swap_z(): return lax.ppermute(value, 'z', [(z, z ^ bit) for z in range(8)])  19.7 us
    ppermute x2, starting transfers between devices, swap_half(): return lax.ppermute(value, 'h', [(0, 1), (1, 0)])  15 us
    all_to_all x2, starting transfers between devices, gather_plane(): return lax.all_to_all(whole, ('x', 'y'), 0, 0, tiled=True)  13.6 us
    ppermute x1, starting transfers between devices, shards(): lax.ppermute(k_rows, ('h', 'z', 'c'), [(i * 16 + j, (1 - i) * 16 + rotate...  9.45 us
    unnamed x34, local copies, waits for them, and re-layouts  9.38 us
  transfers between devices with their start and end apart: 19, of which 12 were waited for; matrix products, arithmetic and copies ran while one was open for 3% of the time, Pallas kernels for 4%

profile of v1, /device:TPU:1, one launch (start us, length us, event | category | flops | bytes accessed | tf_op | source)
XLA Modules:
  0.0 264.9 jit_solution(12787847812732221849)
XLA Ops:
  9.5 23.2 %all_to_all.15 = bf16[8,8,1024]{2,1,0:T(8,128)(2,1)S(1)} all-to-all(bf16[8,8,1024]{2,1,0:T(8,128)(2,1)S(1)} %bitcast.37), channel_id=1, replica_groups=mesh['x'=4,'h'=2,'y'=4,'z'=8,'c'=2] {'z'}, dimensions={0} | all-to-all | bytes 262144 | tf_op jit(solution)/shard_map/out_weight/all_to_all | solution.py:319
  32.7 7.9 %collective-permute-start.14 = (bf16[8,8,1024]{2,1,0:T(8,128)(2,1)S(1)}, bf16[8,8,1024]{2,1,0:T(8,128)(2,1)S(1)}, u32[]{:S(2)}, u32[]{:S(2)}) collective-permute-start(bf16[8,8,1024]{2,1,0:T(8,128)(2,1)S(1)} %all_to_all.15), channel_id=1, source_target_pairs={{0,64},{64,0},{1,65},{65,1},{2,66},{66,2},{3,67},{67,3},{4,68},{68... | collective-permute-start | bytes 393224 | tf_op jit(solution)/shard_map/out_weight/ppermute | solution.py:43
  40.6 11.4 %collective-permute-done.14 = bf16[8,8,1024]{2,1,0:T(8,128)(2,1)S(1)} collective-permute-done((bf16[8,8,1024]{2,1,0:T(8,128)(2,1)S(1)}, bf16[8,8,1024]{2,1,0:T(8,128)(2,1)S(1)}, u32[]{:S(2)}, u32[]{:S(2)}) %collective-permute-start.14) | collective-permute-done | bytes 131104 | tf_op jit(solution)/shard_map/out_weight/ppermute | solution.py:43
  54.4 9.5 %collective-permute-start.7 = (bf16[64,256]{1,0:T(8,128)(2,1)S(1)}, bf16[64,256]{1,0:T(8,128)(2,1)S(1)}, u32[]{:S(2)}, u32[]{:S(2)}) collective-permute-start(bf16[64,256]{1,0:T(8,128)(2,1)S(1)} %bitcast.42), channel_id=1, source_target_pairs={{0,64},{1,66},{2,68},{3,70},{4,72},{5,74},{6,76},{7,78},{8,65},{9,... | collective-permute-start | bytes 98312 | tf_op jit(solution)/shard_map/kv_weight/ppermute | solution.py:307
  63.9 3.7 %collective-permute-start.6 = (bf16[64,256]{1,0:T(8,128)(2,1)S(1)}, bf16[64,256]{1,0:T(8,128)(2,1)S(1)}, u32[]{:S(2)}, u32[]{:S(2)}) collective-permute-start(bf16[64,256]{1,0:T(8,128)(2,1)S(1)} %bitcast.43), channel_id=1, source_target_pairs={{0,0},{1,2},{2,4},{3,6},{4,8},{5,10},{6,12},{7,14},{8,1},{9,3},{10... | collective-permute-start | bytes 98312 | tf_op jit(solution)/shard_map/kv_weight/ppermute | solution.py:306
  67.6 6.1 %collective-permute-done.6 = bf16[64,256]{1,0:T(8,128)(2,1)S(1)} collective-permute-done((bf16[64,256]{1,0:T(8,128)(2,1)S(1)}, bf16[64,256]{1,0:T(8,128)(2,1)S(1)}, u32[]{:S(2)}, u32[]{:S(2)}) %collective-permute-start.6) | collective-permute-done | bytes 32800 | tf_op jit(solution)/shard_map/kv_weight/ppermute | solution.py:306
  74.8 6.8 %all-to-all-start.1 = ((bf16[16,2,64,256]{3,2,1,0:T(8,128)(2,1)}), bf16[16,2,64,256]{3,2,1,0:T(8,128)(2,1)S(1)}, u32[]{:S(2)}, u32[]{:S(2)}) async-start(bf16[16,2,64,256]{3,2,1,0:T(8,128)(2,1)} %broadcast_in_dim.23), calls=%async_computation.1 | async-start | bytes 2097152 | tf_op jit(solution)/shard_map/kv_weight/all_to_all | solution.py:48
  82.6 7.1 %collective-permute-start.5 = (bf16[256,256]{1,0:T(8,128)(2,1)S(1)}, bf16[256,256]{1,0:T(8,128)(2,1)S(1)}, u32[]{:S(2)}, u32[]{:S(2)}) collective-permute-start(bf16[256,256]{1,0:T(8,128)(2,1)S(1)} %get-tuple-element.18), channel_id=1, source_target_pairs={{0,64},{64,0},{1,65},{65,1},{2,66},{66,2},{3,67},{67,3},{4,68},{68... | collective-permute-start | bytes 393224 | tf_op jit(solution)/shard_map/query_weight/ppermute | solution.py:43
  89.7 12.9 %collective-permute-done.5 = bf16[256,256]{1,0:T(8,128)(2,1)S(1)} collective-permute-done((bf16[256,256]{1,0:T(8,128)(2,1)S(1)}, bf16[256,256]{1,0:T(8,128)(2,1)S(1)}, u32[]{:S(2)}, u32[]{:S(2)}) %collective-permute-start.5) | collective-permute-done | bytes 131104 | tf_op jit(solution)/shard_map/query_weight/ppermute | solution.py:43
  105.1 6.8 %all-to-all-start = ((bf16[16,2,256,256]{3,2,1,0:T(8,128)(2,1)}), bf16[16,2,256,256]{3,2,1,0:T(8,128)(2,1)}, u32[]{:S(2)}, u32[]{:S(2)}) async-start(bf16[16,2,256,256]{3,2,1,0:T(8,128)(2,1)} %broadcast_in_dim.22), calls=%async_computation | async-start | bytes 8388608 | tf_op jit(solution)/shard_map/query_weight/all_to_all | solution.py:48
  113.9 14.7 %collective-permute-done = bf16[1,192,512]{2,1,0:T(8,128)(2,1)S(1)} collective-permute-done((bf16[1,192,512]{2,1,0:T(8,128)(2,1)S(1)}, bf16[1,192,512]{2,1,0:T(8,128)(2,1)S(1)}, u32[]{:S(2)}, u32[]{:S(2)}) %collective-permute-start) | collective-permute-done | bytes 196640 | tf_op jit(solution)/shard_map/tokens/ppermute | solution.py:35
  130.6 17.5 %collective-permute-done.1 = bf16[2,192,512]{2,1,0:T(8,128)(2,1)S(1)} collective-permute-done((bf16[2,192,512]{2,1,0:T(8,128)(2,1)S(1)}, bf16[2,192,512]{2,1,0:T(8,128)(2,1)S(1)}, u32[]{:S(2)}, u32[]{:S(2)}) %collective-permute-start.1) | collective-permute-done | bytes 393248 | tf_op jit(solution)/shard_map/tokens/ppermute | solution.py:35
  153.3 15.6 %collective-permute-done.2.far = bf16[4,192,512]{2,1,0:T(8,128)(2,1)S(1)} collective-permute-done((bf16[4,192,512]{2,1,0:T(8,128)(2,1)S(1)}, bf16[4,192,512]{2,1,0:T(8,128)(2,1)S(1)}, u32[]{:S(2)}, u32[]{:S(2)}) %collective-permute-start.2) | collective-permute-done | bytes 786464 | tf_op jit(solution)/shard_map/tokens/ppermute | solution.py:35
  168.9 3.0 %collective-permute-start.4 = (bf16[4,192,512]{2,1,0:T(8,128)(2,1)S(1)}, bf16[4,192,512]{2,1,0:T(8,128)(2,1)S(1)}, u32[]{:S(2)}, u32[]{:S(2)}) collective-permute-start(bf16[4,192,512]{2,1,0:T(8,128)(2,1)S(1)} %collective-permute-done.2.far), channel_id=1, source_target_pairs={{0,1},{1,0},{2,3},{3,2},{4,5},{5,4},{6,7},{7,6},{8,9},{9,8},{10,11... | collective-permute-start | bytes 2359304 | tf_op jit(solution)/shard_map/tokens/ppermute | solution.py:39
  184.8 3.0 %collective-permute-start.8 = (bf16[1,64,192]{2,1,0:T(8,128)(2,1)S(1)}, bf16[1,64,192]{2,1,0:T(8,128)(2,1)S(1)}, u32[]{:S(2)}, u32[]{:S(2)}) collective-permute-start(bf16[1,64,192]{2,1,0:T(8,128)(2,1)S(1)} %bitcast.28), channel_id=1, source_target_pairs={{0,8},{2,10},{4,12},{6,14},{8,0},{10,2},{12,4},{14,6},{1,9},{3,11}... | collective-permute-start | bytes 73736 | tf_op jit(solution)/shard_map/projections/ppermute | solution.py:35
  187.8 7.9 %collective-permute-done.8 = bf16[1,64,192]{2,1,0:T(8,128)(2,1)S(1)} collective-permute-done((bf16[1,64,192]{2,1,0:T(8,128)(2,1)S(1)}, bf16[1,64,192]{2,1,0:T(8,128)(2,1)S(1)}, u32[]{:S(2)}, u32[]{:S(2)}) %collective-permute-start.8) | collective-permute-done | bytes 24608 | tf_op jit(solution)/shard_map/projections/ppermute | solution.py:35
  197.7 4.0 %collective-permute-done.9 = bf16[2,64,192]{2,1,0:T(8,128)(2,1)S(1)} collective-permute-done((bf16[2,64,192]{2,1,0:T(8,128)(2,1)S(1)}, bf16[2,64,192]{2,1,0:T(8,128)(2,1)S(1)}, u32[]{:S(2)}, u32[]{:S(2)}) %collective-permute-start.9) | collective-permute-done | bytes 49184 | tf_op jit(solution)/shard_map/projections/ppermute | solution.py:35
  203.7 3.8 %collective-permute-done.10 = bf16[4,64,192]{2,1,0:T(8,128)(2,1)S(1)} collective-permute-done((bf16[4,64,192]{2,1,0:T(8,128)(2,1)S(1)}, bf16[4,64,192]{2,1,0:T(8,128)(2,1)S(1)}, u32[]{:S(2)}, u32[]{:S(2)}) %collective-permute-start.10) | collective-permute-done | bytes 98336 | tf_op jit(solution)/shard_map/projections/ppermute | solution.py:35
  207.5 3.8 %project_query.1.query = bf16[192,256]{1,0:T(8,128)(2,1)S(1)} custom-call(s32[3]{0:T(128)S(1)} %pad_add_fusion.place.refs_0_, bf16[2,8,192,512]{3,2,1,0:T(8,128)(2,1)S(1)} %norm_tokens.1.normed, bf16[16,2,256,256]{3,2,1,0:T(8,128)(2,1)} %all-to-all-done.weight), custom_call_target="tpu_custom_call" | custom-call | flops 805306368 | bytes 7340032 | tf_op jit(solution)/shard_map/projections/project_query/pallas_call | solution.py:160
  212.4 3.3 %collective-permute-start.11 = (bf16[1,192,256]{2,1,0:T(8,128)(2,1)S(1)}, bf16[1,192,256]{2,1,0:T(8,128)(2,1)S(1)}, u32[]{:S(2)}, u32[]{:S(2)}) collective-permute-start(bf16[1,192,256]{2,1,0:T(8,128)(2,1)S(1)} %bitcast.25), channel_id=1, source_target_pairs={{0,8},{2,10},{4,12},{6,14},{8,0},{10,2},{12,4},{14,6},{1,9},{3,11}... | collective-permute-start | bytes 294920 | tf_op jit(solution)/shard_map/attention/ppermute | solution.py:35
  215.7 13.3 %collective-permute-done.11 = bf16[1,192,256]{2,1,0:T(8,128)(2,1)S(1)} collective-permute-done((bf16[1,192,256]{2,1,0:T(8,128)(2,1)S(1)}, bf16[1,192,256]{2,1,0:T(8,128)(2,1)S(1)}, u32[]{:S(2)}, u32[]{:S(2)}) %collective-permute-start.11) | collective-permute-done | bytes 98336 | tf_op jit(solution)/shard_map/attention/ppermute | solution.py:35
  230.9 8.7 %collective-permute-done.12 = bf16[2,192,256]{2,1,0:T(8,128)(2,1)S(1)} collective-permute-done((bf16[2,192,256]{2,1,0:T(8,128)(2,1)S(1)}, bf16[2,192,256]{2,1,0:T(8,128)(2,1)S(1)}, u32[]{:S(2)}, u32[]{:S(2)}) %collective-permute-start.12) | collective-permute-done | bytes 196640 | tf_op jit(solution)/shard_map/attention/ppermute | solution.py:35
  244.3 7.5 %collective-permute-done.13.refs_2_ = bf16[4,192,256]{2,1,0:T(8,128)(2,1)S(1)} collective-permute-done((bf16[4,192,256]{2,1,0:T(8,128)(2,1)S(1)}, bf16[4,192,256]{2,1,0:T(8,128)(2,1)S(1)}, u32[]{:S(2)}, u32[]{:S(2)}) %collective-permute-start.13) | collective-permute-done | bytes 393248 | tf_op jit(solution)/shard_map/attention/ppermute | solution.py:35
  253.0 3.2 %collective-permute-start.15 = (bf16[192,512]{1,0:T(8,128)(2,1)S(1)}, bf16[192,512]{1,0:T(8,128)(2,1)S(1)}, u32[]{:S(2)}, u32[]{:S(2)}) collective-permute-start(bf16[192,512]{1,0:T(8,128)(2,1)S(1)} %output_other.1), channel_id=1, source_target_pairs={{0,1},{1,0},{2,3},{3,2},{4,5},{5,4},{6,7},{7,6},{8,9},{9,8},{10,11... | collective-permute-start | bytes 589832 | tf_op jit(solution)/shard_map/output/ppermute | solution.py:39
  (74 shorter events, 45.8 us)
Async XLA Ops:
  7.2 74.4 %copy-start.13 = (f32[256,256]{1,0:T(8,128)S(1)}, f32[256,256]{1,0:T(8,128)}, u32[]{:S(2)}) copy-start(f32[256,256]{1,0:T(8,128)} %param.18) | copy-start | bytes 786436
  7.2 74.4 %copy-start.16 = (bf16[256,256]{1,0:T(8,128)(2,1)S(1)}, bf16[256,256]{1,0:T(8,128)(2,1)}, u32[]{:S(2)}) copy-start(bf16[256,256]{1,0:T(8,128)(2,1)} %param.19) | copy-start | bytes 393220
  7.2 74.4 %copy-start.14 = (f32[256,256]{1,0:T(8,128)S(1)}, f32[256,256]{1,0:T(8,128)}, u32[]{:S(2)}) copy-start(f32[256,256]{1,0:T(8,128)} %param.20) | copy-start | bytes 786436
  7.2 74.4 %copy-start.15 = (f32[256,256]{1,0:T(8,128)S(1)}, f32[256,256]{1,0:T(8,128)}, u32[]{:S(2)}) copy-start(f32[256,256]{1,0:T(8,128)} %param.21) | copy-start | bytes 786436
  7.2 234.5 %all-gather.2.cloned.1.call-start = ((), (), s32[]{:S(2)}) async-start(), calls=%async_computation.3 | async-start | bytes 4456448 | tf_op jit(solution)/shard_map/out_weight/all_gather | solution.py:324
  32.7 19.4 %collective-permute-start.14 = (bf16[8,8,1024]{2,1,0:T(8,128)(2,1)S(1)}, bf16[8,8,1024]{2,1,0:T(8,128)(2,1)S(1)}, u32[]{:S(2)}, u32[]{:S(2)}) collective-permute-start(bf16[8,8,1024]{2,1,0:T(8,128)(2,1)S(1)} %all_to_all.15), channel_id=1, source_target_pairs={{0,64},{64,0},{1,65},{65,1},{2,66},{66,2},{3,67},{67,3},{4,68},{68... | collective-permute-start | bytes 393224 | tf_op jit(solution)/shard_map/out_weight/ppermute | solution.py:43
  54.4 13.1 %collective-permute-start.7 = (bf16[64,256]{1,0:T(8,128)(2,1)S(1)}, bf16[64,256]{1,0:T(8,128)(2,1)S(1)}, u32[]{:S(2)}, u32[]{:S(2)}) collective-permute-start(bf16[64,256]{1,0:T(8,128)(2,1)S(1)} %bitcast.42), channel_id=1, source_target_pairs={{0,64},{1,66},{2,68},{3,70},{4,72},{5,74},{6,76},{7,78},{8,65},{9,... | collective-permute-start | bytes 98312 | tf_op jit(solution)/shard_map/kv_weight/ppermute | solution.py:307
  63.9 9.8 %collective-permute-start.6 = (bf16[64,256]{1,0:T(8,128)(2,1)S(1)}, bf16[64,256]{1,0:T(8,128)(2,1)S(1)}, u32[]{:S(2)}, u32[]{:S(2)}) collective-permute-start(bf16[64,256]{1,0:T(8,128)(2,1)S(1)} %bitcast.43), channel_id=1, source_target_pairs={{0,0},{1,2},{2,4},{3,6},{4,8},{5,10},{6,12},{7,14},{8,1},{9,3},{10... | collective-permute-start | bytes 98312 | tf_op jit(solution)/shard_map/kv_weight/ppermute | solution.py:306
  74.8 27.8 %all-to-all-start.1 = ((bf16[16,2,64,256]{3,2,1,0:T(8,128)(2,1)}), bf16[16,2,64,256]{3,2,1,0:T(8,128)(2,1)S(1)}, u32[]{:S(2)}, u32[]{:S(2)}) async-start(bf16[16,2,64,256]{3,2,1,0:T(8,128)(2,1)} %broadcast_in_dim.23), calls=%async_computation.1 | async-start | bytes 2097152 | tf_op jit(solution)/shard_map/kv_weight/all_to_all | solution.py:48
  82.6 20.0 %collective-permute-start.5 = (bf16[256,256]{1,0:T(8,128)(2,1)S(1)}, bf16[256,256]{1,0:T(8,128)(2,1)S(1)}, u32[]{:S(2)}, u32[]{:S(2)}) collective-permute-start(bf16[256,256]{1,0:T(8,128)(2,1)S(1)} %get-tuple-element.18), channel_id=1, source_target_pairs={{0,64},{64,0},{1,65},{65,1},{2,66},{66,2},{3,67},{67,3},{4,68},{68... | collective-permute-start | bytes 393224 | tf_op jit(solution)/shard_map/query_weight/ppermute | solution.py:43
  105.1 69.6 %copy-start.10 = (f32[8192]{0:T(1024)S(1)}, f32[8192]{0:T(1024)}, u32[]{:S(2)}) copy-start(f32[8192]{0:T(1024)} %param.16) | copy-start | bytes 98308
  105.1 102.4 %all-to-all-start = ((bf16[16,2,256,256]{3,2,1,0:T(8,128)(2,1)}), bf16[16,2,256,256]{3,2,1,0:T(8,128)(2,1)}, u32[]{:S(2)}, u32[]{:S(2)}) async-start(bf16[16,2,256,256]{3,2,1,0:T(8,128)(2,1)} %broadcast_in_dim.22), calls=%async_computation | async-start | bytes 8388608 | tf_op jit(solution)/shard_map/query_weight/all_to_all | solution.py:48
  112.0 16.6 %collective-permute-start = (bf16[1,192,512]{2,1,0:T(8,128)(2,1)S(1)}, bf16[1,192,512]{2,1,0:T(8,128)(2,1)S(1)}, u32[]{:S(2)}, u32[]{:S(2)}) collective-permute-start(bf16[1,192,512]{2,1,0:T(8,128)(2,1)S(1)} %bitcast.34), channel_id=1, source_target_pairs={{0,8},{2,10},{4,12},{6,14},{8,0},{10,2},{12,4},{14,6},{1,9},{3,11}... | collective-permute-start | bytes 589832 | tf_op jit(solution)/shard_map/tokens/ppermute | solution.py:35
  128.7 19.5 %collective-permute-start.1 = (bf16[2,192,512]{2,1,0:T(8,128)(2,1)S(1)}, bf16[2,192,512]{2,1,0:T(8,128)(2,1)S(1)}, u32[]{:S(2)}, u32[]{:S(2)}) collective-permute-start(bf16[2,192,512]{2,1,0:T(8,128)(2,1)S(1)} %pad_maximum_fusion.1), channel_id=1, source_target_pairs={{0,4},{2,6},{4,0},{6,2},{8,12},{10,14},{12,8},{14,10},{1,5},{3,7},... | collective-permute-start | bytes 1179656 | tf_op jit(solution)/shard_map/tokens/ppermute | solution.py:35
  148.2 20.7 %collective-permute-start.2 = (bf16[4,192,512]{2,1,0:T(8,128)(2,1)S(1)}, bf16[4,192,512]{2,1,0:T(8,128)(2,1)S(1)}, u32[]{:S(2)}, u32[]{:S(2)}) collective-permute-start(bf16[4,192,512]{2,1,0:T(8,128)(2,1)S(1)} %pad_maximum_fusion.near), channel_id=1, source_target_pairs={{0,2},{2,0},{4,6},{6,4},{8,10},{10,8},{12,14},{14,12},{1,3},{3,1},... | collective-permute-start | bytes 2359304 | tf_op jit(solution)/shard_map/tokens/ppermute | solution.py:35
  150.1 22.8 %collective-permute-start.3 = (bf16[4,192,512]{2,1,0:T(8,128)(2,1)S(1)}, bf16[4,192,512]{2,1,0:T(8,128)(2,1)S(1)}, u32[]{:S(2)}, u32[]{:S(2)}) collective-permute-start(bf16[4,192,512]{2,1,0:T(8,128)(2,1)S(1)} %pad_maximum_fusion.near), channel_id=1, source_target_pairs={{0,1},{1,0},{2,3},{3,2},{4,5},{5,4},{6,7},{7,6},{8,9},{9,8},{10,11... | collective-permute-start | bytes 2359304 | tf_op jit(solution)/shard_map/tokens/ppermute | solution.py:39
  168.9 4.9 %collective-permute-start.4 = (bf16[4,192,512]{2,1,0:T(8,128)(2,1)S(1)}, bf16[4,192,512]{2,1,0:T(8,128)(2,1)S(1)}, u32[]{:S(2)}, u32[]{:S(2)}) collective-permute-start(bf16[4,192,512]{2,1,0:T(8,128)(2,1)S(1)} %collective-permute-done.2.far), channel_id=1, source_target_pairs={{0,1},{1,0},{2,3},{3,2},{4,5},{5,4},{6,7},{7,6},{8,9},{9,8},{10,11... | collective-permute-start | bytes 2359304 | tf_op jit(solution)/shard_map/tokens/ppermute | solution.py:39
  184.8 10.9 %collective-permute-start.8 = (bf16[1,64,192]{2,1,0:T(8,128)(2,1)S(1)}, bf16[1,64,192]{2,1,0:T(8,128)(2,1)S(1)}, u32[]{:S(2)}, u32[]{:S(2)}) collective-permute-start(bf16[1,64,192]{2,1,0:T(8,128)(2,1)S(1)} %bitcast.28), channel_id=1, source_target_pairs={{0,8},{2,10},{4,12},{6,14},{8,0},{10,2},{12,4},{14,6},{1,9},{3,11}... | collective-permute-start | bytes 73736 | tf_op jit(solution)/shard_map/projections/ppermute | solution.py:35
  195.7 6.0 %collective-permute-start.9 = (bf16[2,64,192]{2,1,0:T(8,128)(2,1)S(1)}, bf16[2,64,192]{2,1,0:T(8,128)(2,1)S(1)}, u32[]{:S(2)}, u32[]{:S(2)}) collective-permute-start(bf16[2,64,192]{2,1,0:T(8,128)(2,1)S(1)} %pad_maximum_fusion.8), channel_id=1, source_target_pairs={{0,4},{2,6},{4,0},{6,2},{8,12},{10,14},{12,8},{14,10},{1,5},{3,7},... | collective-permute-start | bytes 147464 | tf_op jit(solution)/shard_map/projections/ppermute | solution.py:35
  201.7 5.7 %collective-permute-start.10 = (bf16[4,64,192]{2,1,0:T(8,128)(2,1)S(1)}, bf16[4,64,192]{2,1,0:T(8,128)(2,1)S(1)}, u32[]{:S(2)}, u32[]{:S(2)}) collective-permute-start(bf16[4,64,192]{2,1,0:T(8,128)(2,1)S(1)} %pad_maximum_fusion.6), channel_id=1, source_target_pairs={{0,2},{2,0},{4,6},{6,4},{8,10},{10,8},{12,14},{14,12},{1,3},{3,1},... | collective-permute-start | bytes 294920 | tf_op jit(solution)/shard_map/projections/ppermute | solution.py:35
  212.4 16.6 %collective-permute-start.11 = (bf16[1,192,256]{2,1,0:T(8,128)(2,1)S(1)}, bf16[1,192,256]{2,1,0:T(8,128)(2,1)S(1)}, u32[]{:S(2)}, u32[]{:S(2)}) collective-permute-start(bf16[1,192,256]{2,1,0:T(8,128)(2,1)S(1)} %bitcast.25), channel_id=1, source_target_pairs={{0,8},{2,10},{4,12},{6,14},{8,0},{10,2},{12,4},{14,6},{1,9},{3,11}... | collective-permute-start | bytes 294920 | tf_op jit(solution)/shard_map/attention/ppermute | solution.py:35
  229.0 10.7 %collective-permute-start.12 = (bf16[2,192,256]{2,1,0:T(8,128)(2,1)S(1)}, bf16[2,192,256]{2,1,0:T(8,128)(2,1)S(1)}, u32[]{:S(2)}, u32[]{:S(2)}) collective-permute-start(bf16[2,192,256]{2,1,0:T(8,128)(2,1)S(1)} %pad_maximum_fusion.5), channel_id=1, source_target_pairs={{0,4},{2,6},{4,0},{6,2},{8,12},{10,14},{12,8},{14,10},{1,5},{3,7},... | collective-permute-start | bytes 589832 | tf_op jit(solution)/shard_map/attention/ppermute | solution.py:35
  239.7 12.1 %collective-permute-start.13 = (bf16[4,192,256]{2,1,0:T(8,128)(2,1)S(1)}, bf16[4,192,256]{2,1,0:T(8,128)(2,1)S(1)}, u32[]{:S(2)}, u32[]{:S(2)}) collective-permute-start(bf16[4,192,256]{2,1,0:T(8,128)(2,1)S(1)} %pad_maximum_fusion.2.refs_1_), channel_id=1, source_target_pairs={{0,2},{2,0},{4,6},{6,4},{8,10},{10,8},{12,14},{14,12},{1,3},{3,1},... | collective-permute-start | bytes 1179656 | tf_op jit(solution)/shard_map/attention/ppermute | solution.py:35
  253.0 4.4 %collective-permute-start.15 = (bf16[192,512]{1,0:T(8,128)(2,1)S(1)}, bf16[192,512]{1,0:T(8,128)(2,1)S(1)}, u32[]{:S(2)}, u32[]{:S(2)}) collective-permute-start(bf16[192,512]{1,0:T(8,128)(2,1)S(1)} %output_other.1), channel_id=1, source_target_pairs={{0,1},{1,0},{2,3},{3,2},{4,5},{5,4},{6,7},{7,6},{8,9},{9,8},{10,11... | collective-permute-start | bytes 589832 | tf_op jit(solution)/shard_map/output/ppermute | solution.py:39
  (12 other events, 45.2 us)
Sparse Core Ops, SparseCore 0:
  52.9 116.8 all-gather.1

commit v2 on v1

v2 whole, which is shorter than its diff:
```python
import jax
import jax.numpy as jnp
from jax import lax
from jax.experimental import pallas as pl
from jax.experimental.pallas import tpu as pltpu
from jax.sharding import Mesh, PartitionSpec as P

HEAD_DIM = 128
ROWS = 192
LANES = 256
MIB = 1 << 20

beta_first = 0.9
beta_second = 0.95
learn_rate = 0.001
adam_eps = 1e-08
norm_eps = 1e-06

ORDER = (0, 4, 2, 6, 1, 5, 3, 7)
BLOCK = (0, 2, 1, 3)

Q_ROWS, KV_ROWS, SUM_ROWS = 192, 64, 16
PART_ROWS = Q_ROWS + KV_ROWS + SUM_ROWS


def adam_step(master, gradient, first, second):
    grad_value = gradient.astype(jnp.float32)
    first = beta_first * first + (1.0 - beta_first) * grad_value
    second = beta_second * second + (1.0 - beta_second) * grad_value * grad_value
    correct_first = 1.0 - beta_first**10
    correct_second = 1.0 - beta_second**10
    master = master - learn_rate * (first / correct_first) / (
        jnp.sqrt(second / correct_second) + adam_eps
    )
    return (master, first, second, master.astype(jnp.bfloat16))


def swap_z(value, bit):
    return lax.ppermute(value, "z", [(z, z ^ bit) for z in range(8)])


def swap_core(value):
    return lax.ppermute(value, "c", [(0, 1), (1, 0)])


def gather_line(pair):
    return [pair] + [swap_z(pair, step) for step in (2, 1, 3)]


def swap_corner(value):
    moves = [(z * 2 + c, (z ^ 4) * 2 + (c ^ 1)) for z in range(8) for c in range(2)]
    return lax.ppermute(value, ("z", "c"), moves)


def swap_bits(value, other_half):
    moves = []
    for x in range(4):
        for h in range(2):
            for y in range(4):
                for z in range(8):
                    for c in range(2):
                        to_x, to_z = (z // 4) * 2 + x % 2, (x // 2) * 4 + z % 4
                        source = (((x * 2 + h) * 4 + y) * 8 + z) * 2 + c
                        half = h ^ other_half
                        target = (((to_x * 2 + half) * 4 + y) * 8 + to_z) * 2 + c
                        moves.append((source, target))
    return lax.ppermute(value, ("x", "h", "y", "z", "c"), moves)


def spread_groups(tokens, y):
    halves = tokens.reshape(ROWS, 2, LANES).transpose(1, 0, 2)
    got = []
    for turn in range(2):
        moves = []
        for at in range(4):
            for c in range(2):
                block = (at % 2) ^ turn
                moves.append((at * 2 + c, (c * 2 + block) * 2 + at // 2))
        piece = jnp.where(y % 2 == 0, halves[turn], halves[1 - turn])
        got.append(lax.ppermute(piece, ("y", "c"), moves))
    return jnp.stack(got)


def gather_columns(value):
    whole = jnp.broadcast_to(value[None], (4,) + value.shape)
    return lax.all_to_all(whole, "x", 0, 0, tiled=True)


def after(value, *others):
    return lax.optimization_barrier((value,) + others)[0]


def vmem(count):
    return [pl.BlockSpec(memory_space=pltpu.VMEM)] * count


def smem():
    return pl.BlockSpec(memory_space=pltpu.SMEM)


def params(mib):
    return pltpu.CompilerParams(vmem_limit_bytes=mib * MIB)


def lanes_of(column):
    wide = jnp.broadcast_to(column, (ROWS, 128))
    wide = jnp.concatenate([wide, jnp.zeros((LANES - ROWS, 128), jnp.float32)])
    return wide.T[0:8]


def split_sum(rows):
    high = rows.astype(jnp.bfloat16)
    low = (rows - high.astype(jnp.float32)).astype(jnp.bfloat16)
    return jnp.concatenate([high, low])


def join_sum(rows):
    rows = rows.astype(jnp.float32)
    return rows[0:8] + rows[8:16]


def gain_kernel(place, gain, own, rest, core_own, core_rest, out, sums):
    z, y = place[0], place[3]
    for other, (first, others) in enumerate(((own, rest), (core_own, core_rest))):
        for turn in range(2):
            total = jnp.zeros((ROWS, LANES), jnp.float32)
            for at in range(4):
                value = first[turn] if at == 0 else others[at - 1, turn]
                value = value.astype(jnp.float32)
                total = total + value * value
                value = value * gain[(z ^ BLOCK[at]) * 4 + y]
                rows = pl.ds((other * 2 + turn) * ROWS, ROWS)
                out[at, rows, :] = value.astype(jnp.bfloat16)
            column = jnp.sum(total, axis=-1, keepdims=True)
            sums[other * 2 + turn] = split_sum(lanes_of(column))


def apply_gain(place, gain, own, rest, core_own, core_rest):
    return pl.pallas_call(
        gain_kernel,
        out_shape=(
            jax.ShapeDtypeStruct((4, 4 * ROWS, LANES), jnp.bfloat16),
            jax.ShapeDtypeStruct((4, SUM_ROWS, LANES), jnp.bfloat16),
        ),
        in_specs=[smem()] + vmem(5),
        out_specs=tuple(vmem(2)),
        compiler_params=params(12),
        cost_estimate=pl.CostEstimate(
            flops=4 * ROWS * 4096, bytes_accessed=3 * MIB, transcendentals=0
        ),
        name="apply_gain",
    )(place, gain, own, rest, core_own, core_rest)


def project_kernel(place, scaled, sums, weight, out):
    z, c, h, y = place[0], place[1], place[2], place[3]
    blocks = []
    for x in range(2):
        for slot in range(2):
            step = (x * 2 + (slot ^ h)) ^ (z & 3)
            blocks.append((x, slot, ((step & 1) * 2) | (step // 2)))
    query = jnp.zeros((4 * ROWS, LANES), jnp.float32)
    for x, slot, at in blocks:
        query = query + jnp.dot(
            scaled[at], weight[x, slot, 0:256, :], preferred_element_type=jnp.float32
        )
    for other in range(2):
        for turn in range(2):
            place_in = other * 2 + turn
            rows = slice(place_in * ROWS, (place_in + 1) * ROWS)
            group = (c ^ other) * 2 + ((y & 1) ^ turn)
            out[group, 0, 0:Q_ROWS, :] = query[rows].astype(jnp.bfloat16)
            total = jnp.zeros((KV_ROWS, ROWS), jnp.float32)
            for x, slot, at in blocks:
                total = total + lax.dot_general(
                    weight[x, slot, 256:320, :],
                    scaled[at, rows, :],
                    (((1,), (1,)), ((), ())),
                    preferred_element_type=jnp.float32,
                )
            total = jnp.concatenate(
                [total, jnp.zeros((KV_ROWS, LANES - ROWS), jnp.float32)], axis=1
            )
            out[group, 0, Q_ROWS : Q_ROWS + KV_ROWS, :] = total.astype(jnp.bfloat16)
            out[group, 0, Q_ROWS + KV_ROWS : PART_ROWS, :] = sums[place_in]


def project(place, scaled, sums, weight):
    return pl.pallas_call(
        project_kernel,
        grid=(2,),
        out_shape=jax.ShapeDtypeStruct((4, 2, PART_ROWS, LANES), jnp.bfloat16),
        in_specs=[
            smem(),
            pl.BlockSpec((4, 4 * ROWS, LANES), lambda i: (0, 0, 0)),
            pl.BlockSpec((4, SUM_ROWS, LANES), lambda i: (0, 0, 0)),
            pl.BlockSpec((2, 2, 320, LANES), lambda i: (i, 0, 0, 0)),
        ],
        out_specs=pl.BlockSpec((4, 1, PART_ROWS, LANES), lambda i: (0, i, 0, 0)),
        compiler_params=params(20),
        cost_estimate=pl.CostEstimate(
            flops=2 * ROWS * 8192 * 320, bytes_accessed=4 * MIB, transcendentals=0
        ),
        name="project",
    )(place, scaled, sums, weight)


def reduce_kernel(place, parts, query, sums, sent, kv_same, kv_other):
    high, c = place[0] // 4, place[1]

    def total(group, start, rows):
        value = jnp.zeros((rows, LANES), jnp.float32)
        for source in range(4):
            value = value + parts[source, group, start : start + rows, :].astype(
                jnp.float32
            )
        return value

    query[...] = total(high, 0, Q_ROWS)
    sent[0:Q_ROWS, :] = total(1 - high, 0, Q_ROWS).astype(jnp.bfloat16)
    squares = join_sum(total(0, Q_ROWS + KV_ROWS, SUM_ROWS))
    sums[...] = squares
    sent[Q_ROWS : Q_ROWS + SUM_ROWS, :] = split_sum(squares)
    kv_same[...] = total(c, Q_ROWS, KV_ROWS).astype(jnp.bfloat16)
    kv_other[...] = total(1 - c, Q_ROWS, KV_ROWS).astype(jnp.bfloat16)


def reduce_parts(place, parts):
    return pl.pallas_call(
        reduce_kernel,
        out_shape=(
            jax.ShapeDtypeStruct((Q_ROWS, LANES), jnp.float32),
            jax.ShapeDtypeStruct((8, LANES), jnp.float32),
            jax.ShapeDtypeStruct((Q_ROWS + SUM_ROWS, LANES), jnp.bfloat16),
            jax.ShapeDtypeStruct((KV_ROWS, LANES), jnp.bfloat16),
            jax.ShapeDtypeStruct((KV_ROWS, LANES), jnp.bfloat16),
        ),
        in_specs=[smem()] + vmem(1),
        out_specs=tuple(vmem(5)),
        compiler_params=params(8),
        cost_estimate=pl.CostEstimate(
            flops=4 * MIB, bytes_accessed=2 * MIB, transcendentals=0
        ),
        name="reduce_parts",
    )(place, parts)


def attend_kernel(
    place, lengths, query, sums, got, p0, p2, p1, p3, out, held
):
    z, c = place[0], place[1]
    squares = sums[...] + join_sum(got[Q_ROWS : Q_ROWS + SUM_ROWS, :])
    scale = lax.rsqrt(squares * (1.0 / 8192) + norm_eps)[0:1, :]
    for step, pair in ((0, p0), (2, p2), (1, p1), (3, p3)):
        for at in range(2):
            piece = pair[at].astype(jnp.float32) * scale
            held[((z & 3) ^ step) * 2 + (c ^ at)] = piece.astype(jnp.bfloat16)
    column = jnp.broadcast_to(scale, (128, LANES)).T[0:ROWS, 0:1]
    heads = query[...] + got[0:Q_ROWS, :].astype(jnp.float32)
    heads = (heads * column).astype(jnp.bfloat16)
    query_at = lax.broadcasted_iota(jnp.int32, (ROWS, LANES), 0)
    key_at = lax.broadcasted_iota(jnp.int32, (ROWS, LANES), 1)
    query_doc = jnp.zeros((ROWS, LANES), jnp.int32)
    key_doc = jnp.zeros((ROWS, LANES), jnp.int32)
    end = 0
    for doc in range(4):
        end = end + lengths[0, doc]
        query_doc = query_doc + (query_at >= end).astype(jnp.int32)
        key_doc = key_doc + (key_at >= end).astype(jnp.int32)
    allowed = (query_doc == key_doc) & (key_at <= query_at)
    for head in range(2):
        keys = held[head * 4 : head * 4 + 4, 0:32, :].reshape(HEAD_DIM, LANES)
        values = held[head * 4 : head * 4 + 4, 32:64, :].reshape(HEAD_DIM, LANES)
        columns = slice(head * HEAD_DIM, (head + 1) * HEAD_DIM)
        scores = jnp.dot(heads[:, columns], keys, preferred_element_type=jnp.float32)
        scores = jnp.where(allowed, scores * HEAD_DIM**-0.5, -1e30)
        scores = scores - jnp.max(scores, axis=-1, keepdims=True)
        weights = jnp.exp(scores)
        weights = weights / jnp.sum(weights, axis=-1, keepdims=True)
        context = lax.dot_general(
            weights.astype(jnp.bfloat16),
            values,
            (((1,), (1,)), ((), ())),
            preferred_element_type=jnp.float32,
        )
        out[:, columns] = context.astype(jnp.bfloat16)


def attend(place, lengths, query, sums, got, pairs):
    return pl.pallas_call(
        attend_kernel,
        out_shape=jax.ShapeDtypeStruct((ROWS, 256), jnp.bfloat16),
        in_specs=[smem(), smem()] + vmem(7),
        out_specs=vmem(1)[0],
        scratch_shapes=[pltpu.VMEM((8, KV_ROWS, LANES), jnp.bfloat16)],
        compiler_params=params(8),
        cost_estimate=pl.CostEstimate(
            flops=8 * ROWS * ROWS * HEAD_DIM,
            bytes_accessed=MIB // 2,
            transcendentals=2 * ROWS * ROWS,
        ),
        name="attend",
    )(place, lengths, query, sums, got, *pairs)


def output_kernel(place, p0, p2, p1, p3, weight, out, *, other):
    start = pl.multiple_of((place[1] ^ other) * 512, 512)
    total = jnp.zeros((ROWS, 512), jnp.float32)
    for at in range(8):
        part = (p0, p2, p1, p3)[at // 2][at % 2]
        total = total + jnp.dot(
            part,
            weight[place[0] ^ ORDER[at], :, pl.ds(start, 512)],
            preferred_element_type=jnp.float32,
        )
    out[...] = total.astype(out.dtype)


def project_output(place, pairs, weight, other):
    def kernel(*refs):
        output_kernel(*refs, other=other)

    return pl.pallas_call(
        kernel,
        out_shape=jax.ShapeDtypeStruct(
            (ROWS, 512), jnp.bfloat16 if other else jnp.float32
        ),
        in_specs=[smem()] + vmem(5),
        out_specs=vmem(1)[0],
        compiler_params=params(24),
        cost_estimate=pl.CostEstimate(
            flops=2 * ROWS * 2048 * 512, bytes_accessed=5 * MIB, transcendentals=0
        ),
        name="output_other" if other else "output_own",
    )(place, *pairs, weight)


def shards(
    tokens,
    norm_gain,
    doc_lengths,
    query_master,
    query_grad,
    query_first,
    query_second,
    kv_master,
    kv_grad,
    kv_first,
    kv_second,
    out_master,
    out_grad,
    out_first,
    out_second,
):
    z, c, h, y = (lax.axis_index(name) for name in ("z", "c", "h", "y"))
    place = jnp.stack([z, c, h, y]).astype(jnp.int32)

    with jax.named_scope("adam"):
        q_master, q_first, q_second, q_weight = adam_step(
            query_master, query_grad, query_first, query_second
        )
        k_master, k_first, k_second, k_weight = adam_step(
            kv_master, kv_grad, kv_first, kv_second
        )
        o_master, o_first, o_second, o_weight = adam_step(
            out_master, out_grad, out_first, out_second
        )

    with jax.named_scope("in_weight"):
        k_rows = k_weight.transpose(0, 2, 1).reshape(KV_ROWS, 256)
        w_rows = jnp.concatenate([q_weight, k_rows])
        w_rows = jnp.stack([swap_bits(w_rows, 0), swap_bits(w_rows, 1)])
        w_whole = gather_columns(w_rows)

    with jax.named_scope("tokens"):
        own = spread_groups(tokens, y)
        core_own = swap_core(own)
        rest = jnp.stack([swap_z(own, step) for step in BLOCK[1:]])
        core_rest = swap_core(rest)
        gain = norm_gain.reshape(32, 1, LANES)
        scaled, sums = apply_gain(place, gain, own, rest, core_own, core_rest)

    with jax.named_scope("out_columns"):
        o_parts = o_weight.reshape(8, 8, 1024).transpose(1, 0, 2)
        o_parts = jnp.broadcast_to(o_parts[None], (2, 8, 8, 1024)).reshape(16, 8, 1024)
        o_parts = lax.all_to_all(o_parts, ("h", "z"), 0, 0, tiled=True)
        o_halves = o_parts.reshape(2, 8, 8, 1024)

    with jax.named_scope("out_weight"):
        o_whole = lax.all_gather(o_halves, ("x", "y"), axis=0, tiled=False)
        o_whole = o_whole.reshape(4, 4, 2, 8, 8, 1024).transpose(3, 0, 2, 1, 4, 5)
        o_whole = o_whole.reshape(8, 256, 1024)

    with jax.named_scope("projections"):
        parts = project(place, scaled, sums, w_whole)
        parts = lax.all_to_all(parts, "y", 0, 0, tiled=True)
        query, sums, sent, kv_same, kv_other = reduce_parts(place, parts)
        same = kv_same.astype(jnp.float32) + swap_z(kv_same, 4).astype(jnp.float32)
        other = swap_core(kv_other).astype(jnp.float32) + swap_corner(
            kv_other
        ).astype(jnp.float32)
        pieces = jnp.stack([same, other]).astype(jnp.bfloat16)
        got = swap_z(after(sent, pieces), 4)
        pieces = gather_line(pieces)

    with jax.named_scope("attention"):
        context = attend(place, doc_lengths, query, sums, got, pieces)
        context = gather_line(jnp.stack([context, swap_z(context, 4)]))

    with jax.named_scope("output"):
        sent = swap_core(project_output(place, context, o_whole, 1))
        kept = project_output(place, context, o_whole, 0)
        mixed = (kept + sent.astype(jnp.float32)).astype(jnp.bfloat16)

    return (
        mixed,
        q_master,
        q_first,
        q_second,
        k_master,
        k_first,
        k_second,
        o_master,
        o_first,
        o_second,
    )


def solution(mesh):
    pool, tp = ("x", "h", "y"), ("z", "c")
    split = Mesh(mesh.devices.reshape(4, 2, 4, 8, 2), ("x", "h", "y", "z", "c"))
    weight = P(pool, tp)
    kv_weight = P(None, pool, tp)
    out_weight = P(tp + pool, None)
    in_specs = (
        (P(pool, tp), P(), P(pool, None))
        + (weight,) * 4
        + (kv_weight,) * 4
        + (out_weight,) * 4
    )
    out_specs = (P(pool, tp),) + (weight,) * 3 + (kv_weight,) * 3 + (out_weight,) * 3
    return jax.shard_map(
        shards, mesh=split, in_specs=in_specs, out_specs=out_specs, check_vma=False
    )
```

time: 266 us -> 225 us (0.85)
  waiting for transfers between devices: 124 us -> 43.3 us
  starting transfers between devices: 70 us -> 97.2 us
  blocking collectives: 23.2 us -> 48 us
  local copies, waits for them, and re-layouts: 15.6 us -> 8.34 us
  Pallas kernels: 11.4 us -> 8.07 us
    ppermute x9 -> x12, waiting for transfers between devices: 93.1 us -> 36.7 us  [swap_z(): return lax.ppermute(value, 'z', [(z, z ^ bit) for z in range(8)])]
    ppermute x4 -> x5, waiting for transfers between devices: 30.5 us -> 5.24 us  [the longest x1 5.23 us: swap_corner(): return lax.ppermute(value, ('z', 'c'), moves)]
    all_to_all x1 -> x2, blocking collectives: 23.2 us -> 48 us  [the longest x1 28.8 us: shards(): o_parts = lax.all_to_all(o_parts, ('h', 'z'), 0, 0, tiled=True)]
    ppermute x9 -> x12, starting transfers between devices: 19.7 us -> 39.5 us  [swap_z(): return lax.ppermute(value, 'z', [(z, z ^ bit) for z in range(8)])]
    all_to_all x2 -> x1, starting transfers between devices: 13.6 us -> 21.2 us  [gather_columns(): return lax.all_to_all(whole, 'x', 0, 0, tiled=True)]
    unnamed x34, local copies, waits for them, and re-layouts: 9.38 us -> 4.5 us
    ppermute x4 -> x5, starting transfers between devices: 28.1 us -> 24 us  [the longest x2 11.9 us: swap_bits(): return lax.ppermute(value, ('x', 'h', 'y', 'z', 'c'), moves)]
    ppermute x3 -> x4, starting transfers between devices: 8.55 us -> 12.4 us  [swap_core(): return lax.ppermute(value, 'c', [(0, 1), (1, 0)])]
  transfers between devices with their start and end apart: 19 -> 23, of which waited for: 12 -> 8; matrix products, arithmetic and copies ran while one was open for 3% -> 3% of each run, Pallas kernels for 4% -> 3%
where the time goes in v2:
time: 225 us; the launch traced here: 224 us
  starting transfers between devices  97.2 us (43%)
  blocking collectives  48 us (21%)
  waiting for transfers between devices  43.3 us (19%)
  between operations  14.6 us (6%)
  local copies, waits for them, and re-layouts  8.34 us (4%)
  Pallas kernels  8.07 us (4%)
  other arithmetic  4.96 us (2%)
    ppermute x12, starting transfers between devices, swap_z(): return lax.ppermute(value, 'z', [(z, z ^ bit) for z in range(8)])  39.5 us
    ppermute x12, waiting for transfers between devices, swap_z(): return lax.ppermute(value, 'z', [(z, z ^ bit) for z in range(8)])  36.7 us
    all_to_all x1, blocking collectives, shards(): o_parts = lax.all_to_all(o_parts, ('h', 'z'), 0, 0, tiled=True)  28.8 us
    all_to_all x1, starting transfers between devices, gather_columns(): return lax.all_to_all(whole, 'x', 0, 0, tiled=True)  21.2 us
    all_to_all x1, blocking collectives, shards(): parts = lax.all_to_all(parts, 'y', 0, 0, tiled=True)  19.2 us
    ppermute x4, starting transfers between devices, swap_core(): return lax.ppermute(value, 'c', [(0, 1), (1, 0)])  12.4 us
    ppermute x2, starting transfers between devices, swap_bits(): return lax.ppermute(value, ('x', 'h', 'y', 'z', 'c'), moves)  11.9 us
    ppermute x2, starting transfers between devices, spread_groups(): got.append(lax.ppermute(piece, ('y', 'c'), moves))  7.95 us
  transfers between devices with their start and end apart: 23, of which 8 were waited for; matrix products, arithmetic and copies ran while one was open for 3% of the time, Pallas kernels for 3%

profile of v2, /device:TPU:1, one launch (start us, length us, event | category | flops | bytes accessed | tf_op | source)
XLA Modules:
  0.0 224.4 jit_solution(15814269575719417264)
XLA Ops:
  9.6 28.8 %all_to_all.15 = bf16[16,8,1024]{2,1,0:T(8,128)(2,1)} all-to-all(bf16[16,8,1024]{2,1,0:T(8,128)(2,1)S(1)} %bitcast.47), channel_id=1, replica_groups=mesh['x'=4,'h'=2,'y'=4,'z'=8,'c'=2] {'h','z'}, dimensions={0} | all-to-all | bytes 524288 | tf_op jit(solution)/shard_map/out_columns/all_to_all | solution.py:386
  40.9 11.2 %collective-permute-start.8 = (bf16[320,256]{1,0:T(8,128)(2,1)S(1)}, bf16[320,256]{1,0:T(8,128)(2,1)S(1)}, u32[]{:S(2)}, u32[]{:S(2)}) collective-permute-start(bf16[320,256]{1,0:T(8,128)(2,1)S(1)} %pad_maximum_fusion.4), channel_id=1, source_target_pairs={{0,64},{1,65},{2,66},{3,67},{4,68},{5,69},{6,70},{7,71},{8,320},{9... | collective-permute-start | bytes 491528 | tf_op jit(solution)/shard_map/in_weight/ppermute | solution.py:67
  52.1 6.0 %collective-permute-start = (bf16[192,256]{1,0:T(8,128)(2,1)S(1)}, bf16[192,256]{1,0:T(8,128)(2,1)S(1)}, u32[]{:S(2)}, u32[]{:S(2)}) collective-permute-start(bf16[192,256]{1,0:T(8,128)(2,1)S(1)} %get-tuple-element.38), channel_id=1, source_target_pairs={{0,0},{1,32},{16,16},{17,48},{32,1},{33,33},{48,17},{49,49},{2,2},... | collective-permute-start | bytes 294920 | tf_op jit(solution)/shard_map/tokens/ppermute | solution.py:80
  61.3 21.2 %all-to-all-start = ((bf16[4,2,320,256]{3,2,1,0:T(8,128)(2,1)}), bf16[4,2,320,256]{3,2,1,0:T(8,128)(2,1)S(1)}, u32[]{:S(2)}, u32[]{:S(2)}) async-start(bf16[4,2,320,256]{3,2,1,0:T(8,128)(2,1)} %broadcast_in_dim.4), calls=%async_computation | async-start | bytes 2621440 | tf_op jit(solution)/shard_map/in_weight/all_to_all | solution.py:86
  84.5 4.3 %collective-permute-start.3 = (bf16[2,192,256]{2,1,0:T(8,128)(2,1)S(1)}, bf16[2,192,256]{2,1,0:T(8,128)(2,1)S(1)}, u32[]{:S(2)}, u32[]{:S(2)}) collective-permute-start(bf16[2,192,256]{2,1,0:T(8,128)(2,1)S(1)} %pad_maximum_fusion.2.own), channel_id=1, source_target_pairs={{0,2},{2,0},{4,6},{6,4},{8,10},{10,8},{12,14},{14,12},{1,3},{3,1},... | collective-permute-start | bytes 589832 | tf_op jit(solution)/shard_map/tokens/ppermute | solution.py:39
  88.8 3.1 %collective-permute-start.4 = (bf16[2,192,256]{2,1,0:T(8,128)(2,1)S(1)}, bf16[2,192,256]{2,1,0:T(8,128)(2,1)S(1)}, u32[]{:S(2)}, u32[]{:S(2)}) collective-permute-start(bf16[2,192,256]{2,1,0:T(8,128)(2,1)S(1)} %pad_maximum_fusion.2.own), channel_id=1, source_target_pairs={{0,6},{2,4},{4,2},{6,0},{8,14},{10,12},{12,10},{14,8},{1,7},{3,5},... | collective-permute-start | bytes 589832 | tf_op jit(solution)/shard_map/tokens/ppermute | solution.py:39
  91.9 5.2 %collective-permute-done.2 = bf16[2,192,256]{2,1,0:T(8,128)(2,1)S(1)} collective-permute-done((bf16[2,192,256]{2,1,0:T(8,128)(2,1)S(1)}, bf16[2,192,256]{2,1,0:T(8,128)(2,1)S(1)}, u32[]{:S(2)}, u32[]{:S(2)}) %collective-permute-start.2) | collective-permute-done | bytes 196640 | tf_op jit(solution)/shard_map/tokens/ppermute | solution.py:39
  97.1 4.3 %collective-permute-done.3 = bf16[2,192,256]{2,1,0:T(8,128)(2,1)S(1)} collective-permute-done((bf16[2,192,256]{2,1,0:T(8,128)(2,1)S(1)}, bf16[2,192,256]{2,1,0:T(8,128)(2,1)S(1)}, u32[]{:S(2)}, u32[]{:S(2)}) %collective-permute-start.3) | collective-permute-done | bytes 196640 | tf_op jit(solution)/shard_map/tokens/ppermute | solution.py:39
  101.5 3.5 %collective-permute-start.6 = (bf16[3,2,192,256]{3,2,1,0:T(8,128)(2,1)S(1)}, bf16[3,2,192,256]{3,2,1,0:T(8,128)(2,1)S(1)}, u32[]{:S(2)}, u32[]{:S(2)}) collective-permute-start(bf16[3,2,192,256]{3,2,1,0:T(8,128)(2,1)S(1)} %pad_maximum_fusion.rest), channel_id=1, source_target_pairs={{0,1},{1,0},{2,3},{3,2},{4,5},{5,4},{6,7},{7,6},{8,9},{9,8},{10,11... | collective-permute-start | bytes 1769480 | tf_op jit(solution)/shard_map/tokens/ppermute | solution.py:43
  113.9 2.7 %project.1 = bf16[4,2,272,256]{3,2,1,0:T(8,128)(2,1)S(1)} custom-call(s32[4]{0:T(128)S(1)} %pad_add_fusion.place.refs_0_, bf16[4,768,256]{2,1,0:T(8,128)(2,1)S(1)} %get-tuple-element.18.scaled, bf16[4,16,256]{2,1,0:T(8,128)(2,1)S(1)} %get-tuple-element.19.sums, bf16[4,2,320,256]{3,2,1,0:T(8,128)(2,1)S(1)} %all-to-all-done.weight), custom_call_target="tpu_custom_call" | custom-call | flops 1006632960 | bytes 4194304 | tf_op jit(solution)/shard_map/projections/project/pallas_call | solution.py:189
  116.6 19.2 %all_to_all.16.parts = bf16[4,2,272,256]{3,2,1,0:T(8,128)(2,1)S(1)} all-to-all(bf16[4,2,272,256]{3,2,1,0:T(8,128)(2,1)S(1)} %project.1), channel_id=1, replica_groups=mesh['x'=4,'h'=2,'y'=4,'z'=8,'c'=2] {'y'}, dimensions={0} | all-to-all | bytes 2228224 | tf_op jit(solution)/shard_map/projections/all_to_all | solution.py:396
  136.5 4.9 %collective-permute-start.9 = (bf16[64,256]{1,0:T(8,128)(2,1)S(1)}, bf16[64,256]{1,0:T(8,128)(2,1)S(1)}, u32[]{:S(2)}, u32[]{:S(2)}) collective-permute-start(bf16[64,256]{1,0:T(8,128)(2,1)S(1)} %get-tuple-element.23), channel_id=1, source_target_pairs={{0,8},{2,10},{4,12},{6,14},{8,0},{10,2},{12,4},{14,6},{1,9},{3,11}... | collective-permute-start | bytes 98312 | tf_op jit(solution)/shard_map/projections/ppermute | solution.py:39
  141.4 3.8 %collective-permute-start.10 = (bf16[64,256]{1,0:T(8,128)(2,1)S(1)}, bf16[64,256]{1,0:T(8,128)(2,1)S(1)}, u32[]{:S(2)}, u32[]{:S(2)}) collective-permute-start(bf16[64,256]{1,0:T(8,128)(2,1)S(1)} %get-tuple-element.24), channel_id=1, source_target_pairs={{0,1},{1,0},{2,3},{3,2},{4,5},{5,4},{6,7},{7,6},{8,9},{9,8},{10,11... | collective-permute-start | bytes 98312 | tf_op jit(solution)/shard_map/projections/ppermute | solution.py:43
  145.1 4.2 %collective-permute-start.11 = (bf16[64,256]{1,0:T(8,128)(2,1)S(1)}, bf16[64,256]{1,0:T(8,128)(2,1)S(1)}, u32[]{:S(2)}, u32[]{:S(2)}) collective-permute-start(bf16[64,256]{1,0:T(8,128)(2,1)S(1)} %get-tuple-element.24), channel_id=1, source_target_pairs={{0,9},{1,8},{2,11},{3,10},{4,13},{5,12},{6,15},{7,14},{8,1},{9,0},... | collective-permute-start | bytes 98312 | tf_op jit(solution)/shard_map/projections/ppermute | solution.py:52
  149.4 5.2 %collective-permute-done.11 = bf16[64,256]{1,0:T(8,128)(2,1)S(1)} collective-permute-done((bf16[64,256]{1,0:T(8,128)(2,1)S(1)}, bf16[64,256]{1,0:T(8,128)(2,1)S(1)}, u32[]{:S(2)}, u32[]{:S(2)}) %collective-permute-start.11) | collective-permute-done | bytes 32800 | tf_op jit(solution)/shard_map/projections/ppermute | solution.py:52
  154.7 4.0 %collective-permute-start.12 = (bf16[208,256]{1,0:T(8,128)(2,1)S(1)}, bf16[208,256]{1,0:T(8,128)(2,1)S(1)}, u32[]{:S(2)}, u32[]{:S(2)}) collective-permute-start(bf16[208,256]{1,0:T(8,128)(2,1)S(1)} %get-tuple-element.25), channel_id=1, source_target_pairs={{0,8},{2,10},{4,12},{6,14},{8,0},{10,2},{12,4},{14,6},{1,9},{3,11}... | collective-permute-start | bytes 319496 | tf_op jit(solution)/shard_map/projections/ppermute | solution.py:39
  158.6 4.7 %collective-permute-start.13 = (bf16[2,64,256]{2,1,0:T(8,128)(2,1)S(1)}, bf16[2,64,256]{2,1,0:T(8,128)(2,1)S(1)}, u32[]{:S(2)}, u32[]{:S(2)}) collective-permute-start(bf16[2,64,256]{2,1,0:T(8,128)(2,1)S(1)} %pad_maximum_fusion.5.p0), channel_id=1, source_target_pairs={{0,4},{2,6},{4,0},{6,2},{8,12},{10,14},{12,8},{14,10},{1,5},{3,7},... | collective-permute-start | bytes 196616 | tf_op jit(solution)/shard_map/projections/ppermute | solution.py:39
  165.3 3.6 %collective-permute-start.15 = (bf16[2,64,256]{2,1,0:T(8,128)(2,1)S(1)}, bf16[2,64,256]{2,1,0:T(8,128)(2,1)S(1)}, u32[]{:S(2)}, u32[]{:S(2)}) collective-permute-start(bf16[2,64,256]{2,1,0:T(8,128)(2,1)S(1)} %pad_maximum_fusion.5.p0), channel_id=1, source_target_pairs={{0,6},{2,4},{4,2},{6,0},{8,14},{10,12},{12,10},{14,8},{1,7},{3,5},... | collective-permute-start | bytes 196616 | tf_op jit(solution)/shard_map/projections/ppermute | solution.py:39
  169.6 6.9 %collective-permute-done.15.p3 = bf16[2,64,256]{2,1,0:T(8,128)(2,1)S(1)} collective-permute-done((bf16[2,64,256]{2,1,0:T(8,128)(2,1)S(1)}, bf16[2,64,256]{2,1,0:T(8,128)(2,1)S(1)}, u32[]{:S(2)}, u32[]{:S(2)}) %collective-permute-start.15) | collective-permute-done | bytes 65568 | tf_op jit(solution)/shard_map/projections/ppermute | solution.py:39
  179.7 13.4 %collective-permute-done.16 = bf16[192,256]{1,0:T(8,128)(2,1)S(1)} collective-permute-done((bf16[192,256]{1,0:T(8,128)(2,1)S(1)}, bf16[192,256]{1,0:T(8,128)(2,1)S(1)}, u32[]{:S(2)}, u32[]{:S(2)}) %collective-permute-start.16) | collective-permute-done | bytes 98336 | tf_op jit(solution)/shard_map/attention/ppermute | solution.py:39
  197.0 5.4 %collective-permute-start.19 = (bf16[2,192,256]{2,1,0:T(8,128)(2,1)S(1)}, bf16[2,192,256]{2,1,0:T(8,128)(2,1)S(1)}, u32[]{:S(2)}, u32[]{:S(2)}) collective-permute-start(bf16[2,192,256]{2,1,0:T(8,128)(2,1)S(1)} %pad_maximum_fusion.3.refs_1_), channel_id=1, source_target_pairs={{0,6},{2,4},{4,2},{6,0},{8,14},{10,12},{12,10},{14,8},{1,7},{3,5},... | collective-permute-start | bytes 589832 | tf_op jit(solution)/shard_map/attention/ppermute | solution.py:39
  202.5 2.6 %copy.28 = bf16[8,4,2,4,8,1024]{5,4,3,2,1,0:T(8,128)(2,1)S(1)} copy(bf16[8,4,2,4,8,1024]{5,4,0,2,3,1:T(8,128)(2,1)} %bitcast.45) | data formatting | bytes 8388608 | tf_op jit(solution)/shard_map/out_weight/transpose | solution.py:391
  205.1 6.2 %collective-permute-done.18.refs_3_ = bf16[2,192,256]{2,1,0:T(8,128)(2,1)S(1)} collective-permute-done((bf16[2,192,256]{2,1,0:T(8,128)(2,1)S(1)}, bf16[2,192,256]{2,1,0:T(8,128)(2,1)S(1)}, u32[]{:S(2)}, u32[]{:S(2)}) %collective-permute-start.18) | collective-permute-done | bytes 196640 | tf_op jit(solution)/shard_map/attention/ppermute | solution.py:39
  212.5 3.2 %collective-permute-start.20 = (bf16[192,512]{1,0:T(8,128)(2,1)S(1)}, bf16[192,512]{1,0:T(8,128)(2,1)S(1)}, u32[]{:S(2)}, u32[]{:S(2)}) collective-permute-start(bf16[192,512]{1,0:T(8,128)(2,1)S(1)} %output_other.1), channel_id=1, source_target_pairs={{0,1},{1,0},{2,3},{3,2},{4,5},{5,4},{6,7},{7,6},{8,9},{9,8},{10,11... | collective-permute-start | bytes 589832 | tf_op jit(solution)/shard_map/output/ppermute | solution.py:43
  (83 shorter events, 32.3 us)
Async XLA Ops:
  7.3 195.2 %all-gather.2.cloned.1.call-start = ((), (), s32[]{:S(2)}) async-start(), calls=%async_computation.3 | async-start | bytes 4456448 | tf_op jit(solution)/shard_map/out_weight/all_gather | solution.py:390
  40.2 19.9 %collective-permute-start.7 = (bf16[320,256]{1,0:T(8,128)(2,1)S(1)}, bf16[320,256]{1,0:T(8,128)(2,1)S(1)}, u32[]{:S(2)}, u32[]{:S(2)}) collective-permute-start(bf16[320,256]{1,0:T(8,128)(2,1)S(1)} %pad_maximum_fusion.4), channel_id=1, source_target_pairs={{0,0},{1,1},{2,2},{3,3},{4,4},{5,5},{6,6},{7,7},{8,256},{9,257},{1... | collective-permute-start | bytes 491528 | tf_op jit(solution)/shard_map/in_weight/ppermute | solution.py:67
  40.9 19.2 %collective-permute-start.8 = (bf16[320,256]{1,0:T(8,128)(2,1)S(1)}, bf16[320,256]{1,0:T(8,128)(2,1)S(1)}, u32[]{:S(2)}, u32[]{:S(2)}) collective-permute-start(bf16[320,256]{1,0:T(8,128)(2,1)S(1)} %pad_maximum_fusion.4), channel_id=1, source_target_pairs={{0,64},{1,65},{2,66},{3,67},{4,68},{5,69},{6,70},{7,71},{8,320},{9... | collective-permute-start | bytes 491528 | tf_op jit(solution)/shard_map/in_weight/ppermute | solution.py:67
  52.1 30.4 %collective-permute-start = (bf16[192,256]{1,0:T(8,128)(2,1)S(1)}, bf16[192,256]{1,0:T(8,128)(2,1)S(1)}, u32[]{:S(2)}, u32[]{:S(2)}) collective-permute-start(bf16[192,256]{1,0:T(8,128)(2,1)S(1)} %get-tuple-element.38), channel_id=1, source_target_pairs={{0,0},{1,32},{16,16},{17,48},{32,1},{33,33},{48,17},{49,49},{2,2},... | collective-permute-start | bytes 294920 | tf_op jit(solution)/shard_map/tokens/ppermute | solution.py:80
  58.2 24.4 %collective-permute-start.1 = (bf16[192,256]{1,0:T(8,128)(2,1)S(1)}, bf16[192,256]{1,0:T(8,128)(2,1)S(1)}, u32[]{:S(2)}, u32[]{:S(2)}) collective-permute-start(bf16[192,256]{1,0:T(8,128)(2,1)S(1)} %get-tuple-element.39), channel_id=1, source_target_pairs={{0,16},{1,48},{16,0},{17,32},{32,17},{33,49},{48,1},{49,33},{2,18}... | collective-permute-start | bytes 294920 | tf_op jit(solution)/shard_map/tokens/ppermute | solution.py:80
  61.3 52.6 %all-to-all-start = ((bf16[4,2,320,256]{3,2,1,0:T(8,128)(2,1)}), bf16[4,2,320,256]{3,2,1,0:T(8,128)(2,1)S(1)}, u32[]{:S(2)}, u32[]{:S(2)}) async-start(bf16[4,2,320,256]{3,2,1,0:T(8,128)(2,1)} %broadcast_in_dim.4), calls=%async_computation | async-start | bytes 2621440 | tf_op jit(solution)/shard_map/in_weight/all_to_all | solution.py:86
  82.6 14.5 %collective-permute-start.2 = (bf16[2,192,256]{2,1,0:T(8,128)(2,1)S(1)}, bf16[2,192,256]{2,1,0:T(8,128)(2,1)S(1)}, u32[]{:S(2)}, u32[]{:S(2)}) collective-permute-start(bf16[2,192,256]{2,1,0:T(8,128)(2,1)S(1)} %pad_maximum_fusion.2.own), channel_id=1, source_target_pairs={{0,4},{2,6},{4,0},{6,2},{8,12},{10,14},{12,8},{14,10},{1,5},{3,7},... | collective-permute-start | bytes 589832 | tf_op jit(solution)/shard_map/tokens/ppermute | solution.py:39
  84.5 16.9 %collective-permute-start.3 = (bf16[2,192,256]{2,1,0:T(8,128)(2,1)S(1)}, bf16[2,192,256]{2,1,0:T(8,128)(2,1)S(1)}, u32[]{:S(2)}, u32[]{:S(2)}) collective-permute-start(bf16[2,192,256]{2,1,0:T(8,128)(2,1)S(1)} %pad_maximum_fusion.2.own), channel_id=1, source_target_pairs={{0,2},{2,0},{4,6},{6,4},{8,10},{10,8},{12,14},{14,12},{1,3},{3,1},... | collective-permute-start | bytes 589832 | tf_op jit(solution)/shard_map/tokens/ppermute | solution.py:39
  88.8 12.6 %collective-permute-start.4 = (bf16[2,192,256]{2,1,0:T(8,128)(2,1)S(1)}, bf16[2,192,256]{2,1,0:T(8,128)(2,1)S(1)}, u32[]{:S(2)}, u32[]{:S(2)}) collective-permute-start(bf16[2,192,256]{2,1,0:T(8,128)(2,1)S(1)} %pad_maximum_fusion.2.own), channel_id=1, source_target_pairs={{0,6},{2,4},{4,2},{6,0},{8,14},{10,12},{12,10},{14,8},{1,7},{3,5},... | collective-permute-start | bytes 589832 | tf_op jit(solution)/shard_map/tokens/ppermute | solution.py:39
  101.5 7.6 %collective-permute-start.6 = (bf16[3,2,192,256]{3,2,1,0:T(8,128)(2,1)S(1)}, bf16[3,2,192,256]{3,2,1,0:T(8,128)(2,1)S(1)}, u32[]{:S(2)}, u32[]{:S(2)}) collective-permute-start(bf16[3,2,192,256]{3,2,1,0:T(8,128)(2,1)S(1)} %pad_maximum_fusion.rest), channel_id=1, source_target_pairs={{0,1},{1,0},{2,3},{3,2},{4,5},{5,4},{6,7},{7,6},{8,9},{9,8},{10,11... | collective-permute-start | bytes 1769480 | tf_op jit(solution)/shard_map/tokens/ppermute | solution.py:43
  105.0 3.3 %collective-permute-start.5 = (bf16[2,192,256]{2,1,0:T(8,128)(2,1)S(1)}, bf16[2,192,256]{2,1,0:T(8,128)(2,1)S(1)}, u32[]{:S(2)}, u32[]{:S(2)}) collective-permute-start(bf16[2,192,256]{2,1,0:T(8,128)(2,1)S(1)} %pad_maximum_fusion.2.own), channel_id=1, source_target_pairs={{0,1},{1,0},{2,3},{3,2},{4,5},{5,4},{6,7},{7,6},{8,9},{9,8},{10,11... | collective-permute-start | bytes 589832 | tf_op jit(solution)/shard_map/tokens/ppermute | solution.py:43
  116.6 59.9 %copy-start.7 = (s32[1,4]{1,0:T(1,128)S(1)}, s32[1,4]{1,0:T(1,128)}, u32[]{:S(2)}) copy-start(s32[1,4]{1,0:T(1,128)} %lengths.1) | copy-start | bytes 52
  136.5 12.9 %collective-permute-start.9 = (bf16[64,256]{1,0:T(8,128)(2,1)S(1)}, bf16[64,256]{1,0:T(8,128)(2,1)S(1)}, u32[]{:S(2)}, u32[]{:S(2)}) collective-permute-start(bf16[64,256]{1,0:T(8,128)(2,1)S(1)} %get-tuple-element.23), channel_id=1, source_target_pairs={{0,8},{2,10},{4,12},{6,14},{8,0},{10,2},{12,4},{14,6},{1,9},{3,11}... | collective-permute-start | bytes 98312 | tf_op jit(solution)/shard_map/projections/ppermute | solution.py:39
  141.4 8.0 %collective-permute-start.10 = (bf16[64,256]{1,0:T(8,128)(2,1)S(1)}, bf16[64,256]{1,0:T(8,128)(2,1)S(1)}, u32[]{:S(2)}, u32[]{:S(2)}) collective-permute-start(bf16[64,256]{1,0:T(8,128)(2,1)S(1)} %get-tuple-element.24), channel_id=1, source_target_pairs={{0,1},{1,0},{2,3},{3,2},{4,5},{5,4},{6,7},{7,6},{8,9},{9,8},{10,11... | collective-permute-start | bytes 98312 | tf_op jit(solution)/shard_map/projections/ppermute | solution.py:43
  145.1 9.5 %collective-permute-start.11 = (bf16[64,256]{1,0:T(8,128)(2,1)S(1)}, bf16[64,256]{1,0:T(8,128)(2,1)S(1)}, u32[]{:S(2)}, u32[]{:S(2)}) collective-permute-start(bf16[64,256]{1,0:T(8,128)(2,1)S(1)} %get-tuple-element.24), channel_id=1, source_target_pairs={{0,9},{1,8},{2,11},{3,10},{4,13},{5,12},{6,15},{7,14},{8,1},{9,0},... | collective-permute-start | bytes 98312 | tf_op jit(solution)/shard_map/projections/ppermute | solution.py:52
  154.7 21.8 %collective-permute-start.12 = (bf16[208,256]{1,0:T(8,128)(2,1)S(1)}, bf16[208,256]{1,0:T(8,128)(2,1)S(1)}, u32[]{:S(2)}, u32[]{:S(2)}) collective-permute-start(bf16[208,256]{1,0:T(8,128)(2,1)S(1)} %get-tuple-element.25), channel_id=1, source_target_pairs={{0,8},{2,10},{4,12},{6,14},{8,0},{10,2},{12,4},{14,6},{1,9},{3,11}... | collective-permute-start | bytes 319496 | tf_op jit(solution)/shard_map/projections/ppermute | solution.py:39
  158.6 10.3 %collective-permute-start.13 = (bf16[2,64,256]{2,1,0:T(8,128)(2,1)S(1)}, bf16[2,64,256]{2,1,0:T(8,128)(2,1)S(1)}, u32[]{:S(2)}, u32[]{:S(2)}) collective-permute-start(bf16[2,64,256]{2,1,0:T(8,128)(2,1)S(1)} %pad_maximum_fusion.5.p0), channel_id=1, source_target_pairs={{0,4},{2,6},{4,0},{6,2},{8,12},{10,14},{12,8},{14,10},{1,5},{3,7},... | collective-permute-start | bytes 196616 | tf_op jit(solution)/shard_map/projections/ppermute | solution.py:39
  163.4 6.2 %collective-permute-start.14 = (bf16[2,64,256]{2,1,0:T(8,128)(2,1)S(1)}, bf16[2,64,256]{2,1,0:T(8,128)(2,1)S(1)}, u32[]{:S(2)}, u32[]{:S(2)}) collective-permute-start(bf16[2,64,256]{2,1,0:T(8,128)(2,1)S(1)} %pad_maximum_fusion.5.p0), channel_id=1, source_target_pairs={{0,2},{2,0},{4,6},{6,4},{8,10},{10,8},{12,14},{14,12},{1,3},{3,1},... | collective-permute-start | bytes 196616 | tf_op jit(solution)/shard_map/projections/ppermute | solution.py:39
  165.3 11.2 %collective-permute-start.15 = (bf16[2,64,256]{2,1,0:T(8,128)(2,1)S(1)}, bf16[2,64,256]{2,1,0:T(8,128)(2,1)S(1)}, u32[]{:S(2)}, u32[]{:S(2)}) collective-permute-start(bf16[2,64,256]{2,1,0:T(8,128)(2,1)S(1)} %pad_maximum_fusion.5.p0), channel_id=1, source_target_pairs={{0,6},{2,4},{4,2},{6,0},{8,14},{10,12},{12,10},{14,8},{1,7},{3,5},... | collective-permute-start | bytes 196616 | tf_op jit(solution)/shard_map/projections/ppermute | solution.py:39
  177.8 15.4 %collective-permute-start.16 = (bf16[192,256]{1,0:T(8,128)(2,1)S(1)}, bf16[192,256]{1,0:T(8,128)(2,1)S(1)}, u32[]{:S(2)}, u32[]{:S(2)}) collective-permute-start(bf16[192,256]{1,0:T(8,128)(2,1)S(1)} %attend.1), channel_id=1, source_target_pairs={{0,8},{2,10},{4,12},{6,14},{8,0},{10,2},{12,4},{14,6},{1,9},{3,11}... | collective-permute-start | bytes 294920 | tf_op jit(solution)/shard_map/attention/ppermute | solution.py:39
  193.2 12.0 %collective-permute-start.17 = (bf16[2,192,256]{2,1,0:T(8,128)(2,1)S(1)}, bf16[2,192,256]{2,1,0:T(8,128)(2,1)S(1)}, u32[]{:S(2)}, u32[]{:S(2)}) collective-permute-start(bf16[2,192,256]{2,1,0:T(8,128)(2,1)S(1)} %pad_maximum_fusion.3.refs_1_), channel_id=1, source_target_pairs={{0,4},{2,6},{4,0},{6,2},{8,12},{10,14},{12,8},{14,10},{1,5},{3,7},... | collective-permute-start | bytes 589832 | tf_op jit(solution)/shard_map/attention/ppermute | solution.py:39
  195.1 16.2 %collective-permute-start.18 = (bf16[2,192,256]{2,1,0:T(8,128)(2,1)S(1)}, bf16[2,192,256]{2,1,0:T(8,128)(2,1)S(1)}, u32[]{:S(2)}, u32[]{:S(2)}) collective-permute-start(bf16[2,192,256]{2,1,0:T(8,128)(2,1)S(1)} %pad_maximum_fusion.3.refs_1_), channel_id=1, source_target_pairs={{0,2},{2,0},{4,6},{6,4},{8,10},{10,8},{12,14},{14,12},{1,3},{3,1},... | collective-permute-start | bytes 589832 | tf_op jit(solution)/shard_map/attention/ppermute | solution.py:39
  197.0 14.3 %collective-permute-start.19 = (bf16[2,192,256]{2,1,0:T(8,128)(2,1)S(1)}, bf16[2,192,256]{2,1,0:T(8,128)(2,1)S(1)}, u32[]{:S(2)}, u32[]{:S(2)}) collective-permute-start(bf16[2,192,256]{2,1,0:T(8,128)(2,1)S(1)} %pad_maximum_fusion.3.refs_1_), channel_id=1, source_target_pairs={{0,6},{2,4},{4,2},{6,0},{8,14},{10,12},{12,10},{14,8},{1,7},{3,5},... | collective-permute-start | bytes 589832 | tf_op jit(solution)/shard_map/attention/ppermute | solution.py:39
  212.5 4.4 %collective-permute-start.20 = (bf16[192,512]{1,0:T(8,128)(2,1)S(1)}, bf16[192,512]{1,0:T(8,128)(2,1)S(1)}, u32[]{:S(2)}, u32[]{:S(2)}) collective-permute-start(bf16[192,512]{1,0:T(8,128)(2,1)S(1)} %output_other.1), channel_id=1, source_target_pairs={{0,1},{1,0},{2,3},{3,2},{4,5},{5,4},{6,7},{7,6},{8,9},{9,8},{10,11... | collective-permute-start | bytes 589832 | tf_op jit(solution)/shard_map/output/ppermute | solution.py:43
  (16 other events, 324.5 us)
Sparse Core Ops, SparseCore 0:
  38.5 79.6 all-gather.1

commit v3 on v2

--- a/solution.py
+++ b/solution.py
@@ -20,7 +20,8 @@
 BLOCK = (0, 2, 1, 3)
 
 Q_ROWS, KV_ROWS, SUM_ROWS = 192, 64, 16
-PART_ROWS = Q_ROWS + KV_ROWS + SUM_ROWS
+KV_START, SUM_START = 2 * Q_ROWS, 2 * Q_ROWS + 2 * KV_ROWS
+PART_ROWS = SUM_START + SUM_ROWS
 
 
 def adam_step(master, gradient, first, second):
@@ -47,23 +48,22 @@
     return [pair] + [swap_z(pair, step) for step in (2, 1, 3)]
 
 
-def swap_corner(value):
-    moves = [(z * 2 + c, (z ^ 4) * 2 + (c ^ 1)) for z in range(8) for c in range(2)]
-    return lax.ppermute(value, ("z", "c"), moves)
-
-
-def swap_bits(value, other_half):
+def swap_line(value, axis, bits):
+    return lax.ppermute(value, axis, [(at, at ^ bits) for at in range(4)])
+
+
+def move_weight(value, flip, turn_core):
     moves = []
     for x in range(4):
         for h in range(2):
             for y in range(4):
                 for z in range(8):
                     for c in range(2):
-                        to_x, to_z = (z // 4) * 2 + x % 2, (x // 2) * 4 + z % 4
+                        to_x, to_c = (c, z // 4) if turn_core else (z // 4, c)
+                        to_x, to_z = to_x * 2 + x % 2, (x // 2) * 4 + z % 4
                         source = (((x * 2 + h) * 4 + y) * 8 + z) * 2 + c
-                        half = h ^ other_half
-                        target = (((to_x * 2 + half) * 4 + y) * 8 + to_z) * 2 + c
-                        moves.append((source, target))
+                        target = (((to_x * 2 + (h ^ flip)) * 4 + y) * 8 + to_z) * 2
+                        moves.append((source, target + to_c))
     return lax.ppermute(value, ("x", "h", "y", "z", "c"), moves)
 
 
@@ -81,11 +81,6 @@
     return jnp.stack(got)
 
 
-def gather_columns(value):
-    whole = jnp.broadcast_to(value[None], (4,) + value.shape)
-    return lax.all_to_all(whole, "x", 0, 0, tiled=True)
-
-
 def after(value, *others):
     return lax.optimization_barrier((value,) + others)[0]
 
@@ -120,19 +115,20 @@
 
 
 def gain_kernel(place, gain, own, rest, core_own, core_rest, out, sums):
-    z, y = place[0], place[3]
+    z, c, y = place[0], place[1], place[3]
     for other, (first, others) in enumerate(((own, rest), (core_own, core_rest))):
         for turn in range(2):
+            group = ((c ^ other) ^ (y // 2)) * 2 + turn
+            rows = pl.ds(pl.multiple_of(group * ROWS, ROWS), ROWS)
             total = jnp.zeros((ROWS, LANES), jnp.float32)
             for at in range(4):
                 value = first[turn] if at == 0 else others[at - 1, turn]
                 value = value.astype(jnp.float32)
                 total = total + value * value
                 value = value * gain[(z ^ BLOCK[at]) * 4 + y]
-                rows = pl.ds((other * 2 + turn) * ROWS, ROWS)
                 out[at, rows, :] = value.astype(jnp.bfloat16)
             column = jnp.sum(total, axis=-1, keepdims=True)
-            sums[other * 2 + turn] = split_sum(lanes_of(column))
+            sums[group] = split_sum(lanes_of(column))
 
 
 def apply_gain(place, gain, own, rest, core_own, core_rest):
@@ -152,28 +148,31 @@
     )(place, gain, own, rest, core_own, core_rest)
 
 
-def project_kernel(place, scaled, sums, weight, out):
-    z, c, h, y = place[0], place[1], place[2], place[3]
-    blocks = []
-    for x in range(2):
-        for slot in range(2):
-            step = (x * 2 + (slot ^ h)) ^ (z & 3)
-            blocks.append((x, slot, ((step & 1) * 2) | (step // 2)))
-    query = jnp.zeros((4 * ROWS, LANES), jnp.float32)
-    for x, slot, at in blocks:
-        query = query + jnp.dot(
-            scaled[at], weight[x, slot, 0:256, :], preferred_element_type=jnp.float32
-        )
-    for other in range(2):
-        for turn in range(2):
-            place_in = other * 2 + turn
-            rows = slice(place_in * ROWS, (place_in + 1) * ROWS)
-            group = (c ^ other) * 2 + ((y & 1) ^ turn)
-            out[group, 0, 0:Q_ROWS, :] = query[rows].astype(jnp.bfloat16)
+def project_kernel(place, scaled, sums, w0, w1, w2, w3, *outs):
+    z, h, x = place[0], place[2], place[4]
+    for part in range(2):
+        columns = (x // 2) ^ part
+        blocks = []
+        for low, weight in enumerate(((w0, w1), (w2, w3))[part]):
+            for slot in range(2):
+                step = (((x & 1) ^ low) * 2 + (slot ^ h)) ^ (z & 3)
+                blocks.append((weight, slot, ((step & 1) * 2) | (step // 2)))
+        query = jnp.zeros((4 * ROWS, LANES), jnp.float32)
+        for weight, slot, at in blocks:
+            query = query + jnp.dot(
+                scaled[at], weight[slot, 0:256, :], preferred_element_type=jnp.float32
+            )
+        q_rows = pl.ds(pl.multiple_of(columns * Q_ROWS, Q_ROWS), Q_ROWS)
+        kv_rows = pl.ds(
+            pl.multiple_of(KV_START + columns * KV_ROWS, KV_ROWS), KV_ROWS
+        )
+        for group, out in enumerate(outs):
+            rows = slice(group * ROWS, (group + 1) * ROWS)
+            out[q_rows, :] = query[rows].astype(jnp.bfloat16)
             total = jnp.zeros((KV_ROWS, ROWS), jnp.float32)
-            for x, slot, at in blocks:
+            for weight, slot, at in blocks:
                 total = total + lax.dot_general(
-                    weight[x, slot, 256:320, :],
+                    weight[slot, 256:320, :],
                     scaled[at, rows, :],
                     (((1,), (1,)), ((), ())),
                     preferred_element_type=jnp.float32,
@@ -181,48 +180,43 @@
             total = jnp.concatenate(
                 [total, jnp.zeros((KV_ROWS, LANES - ROWS), jnp.float32)], axis=1
             )
-            out[group, 0, Q_ROWS : Q_ROWS + KV_ROWS, :] = total.astype(jnp.bfloat16)
-            out[group, 0, Q_ROWS + KV_ROWS : PART_ROWS, :] = sums[place_in]
-
-
-def project(place, scaled, sums, weight):
+            out[kv_rows, :] = total.astype(jnp.bfloat16)
+    for group, out in enumerate(outs):
+        out[SUM_START:PART_ROWS, :] = sums[group]
+
+
+def project(place, scaled, sums, weights):
+    part = jax.ShapeDtypeStruct((PART_ROWS, LANES), jnp.bfloat16)
     return pl.pallas_call(
         project_kernel,
-        grid=(2,),
-        out_shape=jax.ShapeDtypeStruct((4, 2, PART_ROWS, LANES), jnp.bfloat16),
-        in_specs=[
-            smem(),
-            pl.BlockSpec((4, 4 * ROWS, LANES), lambda i: (0, 0, 0)),
-            pl.BlockSpec((4, SUM_ROWS, LANES), lambda i: (0, 0, 0)),
-            pl.BlockSpec((2, 2, 320, LANES), lambda i: (i, 0, 0, 0)),
-        ],
-        out_specs=pl.BlockSpec((4, 1, PART_ROWS, LANES), lambda i: (0, i, 0, 0)),
-        compiler_params=params(20),
+        out_shape=(part,) * 4,
+        in_specs=[smem()] + vmem(6),
+        out_specs=tuple(vmem(4)),
+        compiler_params=params(16),
         cost_estimate=pl.CostEstimate(
             flops=2 * ROWS * 8192 * 320, bytes_accessed=4 * MIB, transcendentals=0
         ),
         name="project",
-    )(place, scaled, sums, weight)
-
-
-def reduce_kernel(place, parts, query, sums, sent, kv_same, kv_other):
-    high, c = place[0] // 4, place[1]
-
-    def total(group, start, rows):
+    )(place, scaled, sums, *weights)
+
+
+def reduce_kernel(place, p0, p1, p2, p3, query, sums, sent, kv):
+    high = place[0] // 4
+
+    def total(start, rows):
+        if not isinstance(start, int):
+            start = pl.multiple_of(start, rows)
         value = jnp.zeros((rows, LANES), jnp.float32)
-        for source in range(4):
-            value = value + parts[source, group, start : start + rows, :].astype(
-                jnp.float32
-            )
+        for part in (p0, p1, p2, p3):
+            value = value + part[pl.ds(start, rows), :].astype(jnp.float32)
         return value
 
-    query[...] = total(high, 0, Q_ROWS)
-    sent[0:Q_ROWS, :] = total(1 - high, 0, Q_ROWS).astype(jnp.bfloat16)
-    squares = join_sum(total(0, Q_ROWS + KV_ROWS, SUM_ROWS))
+    kv[...] = total(KV_START, 2 * KV_ROWS).astype(jnp.bfloat16)
+    query[...] = total(high * Q_ROWS, Q_ROWS)
+    sent[0:Q_ROWS, :] = total((1 - high) * Q_ROWS, Q_ROWS).astype(jnp.bfloat16)
+    squares = join_sum(total(SUM_START, SUM_ROWS))
     sums[...] = squares
     sent[Q_ROWS : Q_ROWS + SUM_ROWS, :] = split_sum(squares)
-    kv_same[...] = total(c, Q_ROWS, KV_ROWS).astype(jnp.bfloat16)
-    kv_other[...] = total(1 - c, Q_ROWS, KV_ROWS).astype(jnp.bfloat16)
 
 
 def reduce_parts(place, parts):
@@ -232,29 +226,29 @@
             jax.ShapeDtypeStruct((Q_ROWS, LANES), jnp.float32),
             jax.ShapeDtypeStruct((8, LANES), jnp.float32),
             jax.ShapeDtypeStruct((Q_ROWS + SUM_ROWS, LANES), jnp.bfloat16),
-            jax.ShapeDtypeStruct((KV_ROWS, LANES), jnp.bfloat16),
-            jax.ShapeDtypeStruct((KV_ROWS, LANES), jnp.bfloat16),
-        ),
-        in_specs=[smem()] + vmem(1),
-        out_specs=tuple(vmem(5)),
+            jax.ShapeDtypeStruct((2 * KV_ROWS, LANES), jnp.bfloat16),
+        ),
+        in_specs=[smem()] + vmem(4),
+        out_specs=tuple(vmem(4)),
         compiler_params=params(8),
         cost_estimate=pl.CostEstimate(
             flops=4 * MIB, bytes_accessed=2 * MIB, transcendentals=0
         ),
         name="reduce_parts",
-    )(place, parts)
+    )(place, *parts)
 
 
 def attend_kernel(
     place, lengths, query, sums, got, p0, p2, p1, p3, out, held
 ):
-    z, c = place[0], place[1]
+    z = place[0]
     squares = sums[...] + join_sum(got[Q_ROWS : Q_ROWS + SUM_ROWS, :])
     scale = lax.rsqrt(squares * (1.0 / 8192) + norm_eps)[0:1, :]
     for step, pair in ((0, p0), (2, p2), (1, p1), (3, p3)):
         for at in range(2):
-            piece = pair[at].astype(jnp.float32) * scale
-            held[((z & 3) ^ step) * 2 + (c ^ at)] = piece.astype(jnp.bfloat16)
+            piece = pair[at * KV_ROWS : (at + 1) * KV_ROWS, :]
+            piece = piece.astype(jnp.float32) * scale
+            held[((z & 3) ^ step) * 2 + at] = piece.astype(jnp.bfloat16)
     column = jnp.broadcast_to(scale, (128, LANES)).T[0:ROWS, 0:1]
     heads = query[...] + got[0:Q_ROWS, :].astype(jnp.float32)
     heads = (heads * column).astype(jnp.bfloat16)
@@ -352,8 +346,9 @@
     out_first,
     out_second,
 ):
-    z, c, h, y = (lax.axis_index(name) for name in ("z", "c", "h", "y"))
-    place = jnp.stack([z, c, h, y]).astype(jnp.int32)
+    place = [lax.axis_index(name) for name in ("z", "c", "h", "y", "x")]
+    y = place[3]
+    place = jnp.stack(place).astype(jnp.int32)
 
     with jax.named_scope("adam"):
         q_master, q_first, q_second, q_weight = adam_step(
@@ -368,40 +363,44 @@
 
     with jax.named_scope("in_weight"):
         k_rows = k_weight.transpose(0, 2, 1).reshape(KV_ROWS, 256)
-        w_rows = jnp.concatenate([q_weight, k_rows])
-        w_rows = jnp.stack([swap_bits(w_rows, 0), swap_bits(w_rows, 1)])
-        w_whole = gather_columns(w_rows)
+        weights = [
+            jnp.concatenate([move_weight(q_weight, flip, 0), move_weight(k_rows, flip, 1)])
+            for flip in range(2)
+        ]
+        weights = jnp.stack(weights)
 
     with jax.named_scope("tokens"):
         own = spread_groups(tokens, y)
         core_own = swap_core(own)
-        rest = jnp.stack([swap_z(own, step) for step in BLOCK[1:]])
-        core_rest = swap_core(rest)
+        moved = after(own, weights)
+        rest = jnp.stack([swap_z(moved, step) for step in BLOCK[1:]])
+        weights = [weights] + [swap_line(weights, "x", bits) for bits in (1, 2, 3)]
+        core_rest = swap_core(after(rest, *weights))
         gain = norm_gain.reshape(32, 1, LANES)
-        scaled, sums = apply_gain(place, gain, own, rest, core_own, core_rest)
+        scaled, sums = apply_gain(
+            place, gain, own, rest, core_own, core_rest
+        )
+
+    with jax.named_scope("projections"):
+        parts = project(place, scaled, sums, weights)
+        parts = [parts[0]] + [swap_line(parts[n], "y", n) for n in (1, 2, 3)]
+        query, sums, sent, kv = reduce_parts(place, parts)
+        kv = kv.astype(jnp.float32) + swap_z(kv, 4).astype(jnp.float32)
+        kv = kv.astype(jnp.bfloat16)
+        got = swap_z(after(sent, kv), 4)
+        pieces = gather_line(kv)
 
     with jax.named_scope("out_columns"):
-        o_parts = o_weight.reshape(8, 8, 1024).transpose(1, 0, 2)
-        o_parts = jnp.broadcast_to(o_parts[None], (2, 8, 8, 1024)).reshape(16, 8, 1024)
-        o_parts = lax.all_to_all(o_parts, ("h", "z"), 0, 0, tiled=True)
-        o_halves = o_parts.reshape(2, 8, 8, 1024)
+        o_rows = lax.all_gather(after(o_weight, weights[0]), ("h", "z"), axis=0, tiled=False)
+        start = lax.axis_index("z") * 1024
+        o_rows = after(o_rows, query)
+        o_halves = lax.dynamic_slice_in_dim(o_rows, start, 1024, axis=2)
+        o_halves = o_halves.reshape(2, 8, 8, 1024)
 
     with jax.named_scope("out_weight"):
         o_whole = lax.all_gather(o_halves, ("x", "y"), axis=0, tiled=False)
         o_whole = o_whole.reshape(4, 4, 2, 8, 8, 1024).transpose(3, 0, 2, 1, 4, 5)
         o_whole = o_whole.reshape(8, 256, 1024)
-
-    with jax.named_scope("projections"):
-        parts = project(place, scaled, sums, w_whole)
-        parts = lax.all_to_all(parts, "y", 0, 0, tiled=True)
-        query, sums, sent, kv_same, kv_other = reduce_parts(place, parts)
-        same = kv_same.astype(jnp.float32) + swap_z(kv_same, 4).astype(jnp.float32)
-        other = swap_core(kv_other).astype(jnp.float32) + swap_corner(
-            kv_other
-        ).astype(jnp.float32)
-        pieces = jnp.stack([same, other]).astype(jnp.bfloat16)
-        got = swap_z(after(sent, pieces), 4)
-        pieces = gather_line(pieces)
 
     with jax.named_scope("attention"):
         context = attend(place, doc_lengths, query, sums, got, pieces)

time: 225 us -> 214 us (0.951)
  blocking collectives: 48 us -> 0 us
  starting transfers between devices: 97.2 us -> 123 us
  waiting for transfers between devices: 43.3 us -> 57.8 us
  local copies, waits for them, and re-layouts: 8.34 us -> 4.45 us
    ppermute x3 -> x10, starting transfers between devices: 16.1 us -> 66.5 us  [the longest x4 33.5 us: move_weight(): return lax.ppermute(value, ('x', 'h', 'y', 'z', 'c'), moves)]
    all_to_all x2 -> x0, blocking collectives: 48 us -> none  [the longest x1 28.8 us: shards(): o_parts = lax.all_to_all(o_parts, ('h', 'z'), 0, 0, tiled=True)]
    all_to_all x1 -> x0, starting transfers between devices: 21.2 us -> none  [gather_columns(): return lax.all_to_all(whole, 'x', 0, 0, tiled=True)]
    ppermute x3 -> x10, waiting for transfers between devices: 5.23 us -> 12.5 us  [the longest x6 11.2 us: swap_line(): return lax.ppermute(value, axis, [(at, at ^ bits) for at in range(4)])]
    ppermute x4 -> x3, starting transfers between devices: 12.4 us -> 6.85 us  [swap_core(): return lax.ppermute(value, 'c', [(0, 1), (1, 0)])]
    unnamed x34 -> x14, local copies, waits for them, and re-layouts: 4.5 us -> 0.03 us
    all_gather x1, waiting for transfers between devices: 0.02 us -> 3.59 us  [shards(): o_whole = lax.all_gather(o_halves, ('x', 'y'), axis=0, tiled=False)]
    ppermute x12, starting transfers between devices: 39.5 us -> 42 us  [swap_z(): return lax.ppermute(value, 'z', [(z, z ^ bit) for z in range(8)])]
  transfers between devices with their start and end apart: 23 -> 29, of which waited for: 8 -> 15; matrix products, arithmetic and copies ran while one was open for 3% -> 3% of each run, Pallas kernels for 3% -> 3%
where the time goes in v3:
time: 214 us; the launch traced here: 213 us
  starting transfers between devices  123 us (57%)
  waiting for transfers between devices  57.8 us (27%)
  between operations  14.5 us (7%)
  Pallas kernels  7.84 us (4%)
  other arithmetic  5.78 us (3%)
  local copies, waits for them, and re-layouts  4.45 us (2%)
    ppermute x12, starting transfers between devices, swap_z(): return lax.ppermute(value, 'z', [(z, z ^ bit) for z in range(8)])  42 us
    ppermute x12, waiting for transfers between devices, swap_z(): return lax.ppermute(value, 'z', [(z, z ^ bit) for z in range(8)])  38.4 us
    ppermute x4, starting transfers between devices, move_weight(): return lax.ppermute(value, ('x', 'h', 'y', 'z', 'c'), moves)  33.5 us
    ppermute x6, starting transfers between devices, swap_line(): return lax.ppermute(value, axis, [(at, at ^ bits) for at in range(4)])  33 us
    ppermute x6, waiting for transfers between devices, swap_line(): return lax.ppermute(value, axis, [(at, at ^ bits) for at in range(4)])  11.2 us
    ppermute x2, starting transfers between devices, spread_groups(): got.append(lax.ppermute(piece, ('y', 'c'), moves))  7.18 us
    ppermute x3, starting transfers between devices, swap_core(): return lax.ppermute(value, 'c', [(0, 1), (1, 0)])  6.85 us
    convert_element_type x3, other arithmetic, adam_step(): return (master, first, second, master.astype(jnp.bfloat16))  4.86 us
  transfers between devices with their start and end apart: 29, of which 15 were waited for; matrix products, arithmetic and copies ran while one was open for 3% of the time, Pallas kernels for 3%

profile of v3, /device:TPU:1, one launch (start us, length us, event | category | flops | bytes accessed | tf_op | source)
XLA Modules:
  0.0 212.9 jit_solution(6412805303232510289)
XLA Ops:
  10.3 16.3 %collective-permute-start.4 = (bf16[256,256]{1,0:T(8,128)(2,1)S(1)}, bf16[256,256]{1,0:T(8,128)(2,1)S(1)}, u32[]{:S(2)}, u32[]{:S(2)}) collective-permute-start(bf16[256,256]{1,0:T(8,128)(2,1)S(1)} %get-tuple-element.44), channel_id=1, source_target_pairs={{0,64},{1,65},{2,66},{3,67},{4,68},{5,69},{6,70},{7,71},{8,320},{9... | collective-permute-start | bytes 393224 | tf_op jit(solution)/shard_map/in_weight/ppermute | solution.py:67
  28.2 9.7 %collective-permute-start.3 = (bf16[64,256]{1,0:T(8,128)(2,1)S(1)}, bf16[64,256]{1,0:T(8,128)(2,1)S(1)}, u32[]{:S(2)}, u32[]{:S(2)}) collective-permute-start(bf16[64,256]{1,0:T(8,128)(2,1)S(1)} %bitcast.51), channel_id=1, source_target_pairs={{0,0},{1,256},{2,2},{3,258},{4,4},{5,260},{6,6},{7,262},{8,1},{9,2... | collective-permute-start | bytes 98312 | tf_op jit(solution)/shard_map/in_weight/ppermute | solution.py:67
  37.9 6.7 %collective-permute-start.5 = (bf16[64,256]{1,0:T(8,128)(2,1)S(1)}, bf16[64,256]{1,0:T(8,128)(2,1)S(1)}, u32[]{:S(2)}, u32[]{:S(2)}) collective-permute-start(bf16[64,256]{1,0:T(8,128)(2,1)S(1)} %bitcast.52), channel_id=1, source_target_pairs={{0,64},{1,320},{2,66},{3,322},{4,68},{5,324},{6,70},{7,326},{8,65}... | collective-permute-start | bytes 98312 | tf_op jit(solution)/shard_map/in_weight/ppermute | solution.py:67
  49.2 5.3 %collective-permute-start = (bf16[192,256]{1,0:T(8,128)(2,1)S(1)}, bf16[192,256]{1,0:T(8,128)(2,1)S(1)}, u32[]{:S(2)}, u32[]{:S(2)}) collective-permute-start(bf16[192,256]{1,0:T(8,128)(2,1)S(1)} %get-tuple-element.52), channel_id=1, source_target_pairs={{0,0},{1,32},{16,16},{17,48},{32,1},{33,33},{48,17},{49,49},{2,2},... | collective-permute-start | bytes 294920 | tf_op jit(solution)/shard_map/tokens/ppermute | solution.py:80
  56.7 3.1 %collective-permute-start.6 = (bf16[2,192,256]{2,1,0:T(8,128)(2,1)S(1)}, bf16[2,192,256]{2,1,0:T(8,128)(2,1)S(1)}, u32[]{:S(2)}, u32[]{:S(2)}) collective-permute-start(bf16[2,192,256]{2,1,0:T(8,128)(2,1)S(1)} %pad_maximum_fusion.2.own), channel_id=1, source_target_pairs={{0,4},{2,6},{4,0},{6,2},{8,12},{10,14},{12,8},{14,10},{1,5},{3,7},... | collective-permute-start | bytes 589832 | tf_op jit(solution)/shard_map/tokens/ppermute | solution.py:40
  59.9 3.0 %collective-permute-start.10 = (bf16[2,320,256]{2,1,0:T(8,128)(2,1)S(1)}, bf16[2,320,256]{2,1,0:T(8,128)(2,1)S(1)}, u32[]{:S(2)}, u32[]{:S(2)}) collective-permute-start(bf16[2,320,256]{2,1,0:T(8,128)(2,1)S(1)} %pad_maximum_fusion.1.w0), channel_id=1, source_target_pairs={{0,128},{128,0},{256,384},{384,256},{1,129},{129,1},{257,385},{385... | collective-permute-start | bytes 983048 | tf_op jit(solution)/shard_map/tokens/ppermute | solution.py:52
  62.9 18.5 %collective-permute-start.11 = (bf16[2,320,256]{2,1,0:T(8,128)(2,1)S(1)}, bf16[2,320,256]{2,1,0:T(8,128)(2,1)S(1)}, u32[]{:S(2)}, u32[]{:S(2)}) collective-permute-start(bf16[2,320,256]{2,1,0:T(8,128)(2,1)S(1)} %pad_maximum_fusion.1.w0), channel_id=1, source_target_pairs={{0,256},{128,384},{256,0},{384,128},{1,257},{129,385},{257,1},{385... | collective-permute-start | bytes 983048 | tf_op jit(solution)/shard_map/tokens/ppermute | solution.py:52
  85.3 5.4 %collective-permute-start.8 = (bf16[2,192,256]{2,1,0:T(8,128)(2,1)S(1)}, bf16[2,192,256]{2,1,0:T(8,128)(2,1)S(1)}, u32[]{:S(2)}, u32[]{:S(2)}) collective-permute-start(bf16[2,192,256]{2,1,0:T(8,128)(2,1)S(1)} %pad_maximum_fusion.2.own), channel_id=1, source_target_pairs={{0,6},{2,4},{4,2},{6,0},{8,14},{10,12},{12,10},{14,8},{1,7},{3,5},... | collective-permute-start | bytes 589832 | tf_op jit(solution)/shard_map/tokens/ppermute | solution.py:40
  92.3 8.3 %collective-permute-done.8 = bf16[2,192,256]{2,1,0:T(8,128)(2,1)S(1)} collective-permute-done((bf16[2,192,256]{2,1,0:T(8,128)(2,1)S(1)}, bf16[2,192,256]{2,1,0:T(8,128)(2,1)S(1)}, u32[]{:S(2)}, u32[]{:S(2)}) %collective-permute-start.8) | collective-permute-done | bytes 196640 | tf_op jit(solution)/shard_map/tokens/ppermute | solution.py:40
  109.7 2.8 %collective-permute-start.14 = (bf16[528,256]{1,0:T(8,128)(2,1)S(1)}, bf16[528,256]{1,0:T(8,128)(2,1)S(1)}, u32[]{:S(2)}, u32[]{:S(2)}) collective-permute-start(bf16[528,256]{1,0:T(8,128)(2,1)S(1)} %get-tuple-element.30), channel_id=1, source_target_pairs={{0,16},{16,0},{32,48},{48,32},{1,17},{17,1},{33,49},{49,33},{2,18}... | collective-permute-start | bytes 811016 | tf_op jit(solution)/shard_map/projections/ppermute | solution.py:52
  114.5 4.9 %collective-permute-start.16 = (bf16[528,256]{1,0:T(8,128)(2,1)S(1)}, bf16[528,256]{1,0:T(8,128)(2,1)S(1)}, u32[]{:S(2)}, u32[]{:S(2)}) collective-permute-start(bf16[528,256]{1,0:T(8,128)(2,1)S(1)} %get-tuple-element.32), channel_id=1, source_target_pairs={{0,48},{16,32},{32,16},{48,0},{1,49},{17,33},{33,17},{49,1},{2,50}... | collective-permute-start | bytes 811016 | tf_op jit(solution)/shard_map/projections/ppermute | solution.py:52
  119.4 4.4 %collective-permute-done.15.p2 = bf16[528,256]{1,0:T(8,128)(2,1)S(1)} collective-permute-done((bf16[528,256]{1,0:T(8,128)(2,1)S(1)}, bf16[528,256]{1,0:T(8,128)(2,1)S(1)}, u32[]{:S(2)}, u32[]{:S(2)}) %collective-permute-start.15) | collective-permute-done | bytes 270368 | tf_op jit(solution)/shard_map/projections/ppermute | solution.py:52
  123.9 6.6 %collective-permute-done.16.p3 = bf16[528,256]{1,0:T(8,128)(2,1)S(1)} collective-permute-done((bf16[528,256]{1,0:T(8,128)(2,1)S(1)}, bf16[528,256]{1,0:T(8,128)(2,1)S(1)}, u32[]{:S(2)}, u32[]{:S(2)}) %collective-permute-start.16) | collective-permute-done | bytes 270368 | tf_op jit(solution)/shard_map/projections/ppermute | solution.py:52
  132.9 5.9 %collective-permute-start.17 = (bf16[128,256]{1,0:T(8,128)(2,1)S(1)}, bf16[128,256]{1,0:T(8,128)(2,1)S(1)}, u32[]{:S(2)}, u32[]{:S(2)}) collective-permute-start(bf16[128,256]{1,0:T(8,128)(2,1)S(1)} %get-tuple-element.36), channel_id=1, source_target_pairs={{0,8},{2,10},{4,12},{6,14},{8,0},{10,2},{12,4},{14,6},{1,9},{3,11}... | collective-permute-start | bytes 196616 | tf_op jit(solution)/shard_map/projections/ppermute | solution.py:40
  138.9 7.6 %collective-permute-done.17 = bf16[128,256]{1,0:T(8,128)(2,1)S(1)} collective-permute-done((bf16[128,256]{1,0:T(8,128)(2,1)S(1)}, bf16[128,256]{1,0:T(8,128)(2,1)S(1)}, u32[]{:S(2)}, u32[]{:S(2)}) %collective-permute-start.17) | collective-permute-done | bytes 65568 | tf_op jit(solution)/shard_map/projections/ppermute | solution.py:40
  148.5 6.4 %collective-permute-start.19 = (bf16[128,256]{1,0:T(8,128)(2,1)S(1)}, bf16[128,256]{1,0:T(8,128)(2,1)S(1)}, u32[]{:S(2)}, u32[]{:S(2)}) collective-permute-start(bf16[128,256]{1,0:T(8,128)(2,1)S(1)} %add_convert_fusion.1.p0), channel_id=1, source_target_pairs={{0,4},{2,6},{4,0},{6,2},{8,12},{10,14},{12,8},{14,10},{1,5},{3,7},... | collective-permute-start | bytes 196616 | tf_op jit(solution)/shard_map/projections/ppermute | solution.py:40
  156.9 3.1 %collective-permute-start.21 = (bf16[128,256]{1,0:T(8,128)(2,1)S(1)}, bf16[128,256]{1,0:T(8,128)(2,1)S(1)}, u32[]{:S(2)}, u32[]{:S(2)}) collective-permute-start(bf16[128,256]{1,0:T(8,128)(2,1)S(1)} %add_convert_fusion.1.p0), channel_id=1, source_target_pairs={{0,6},{2,4},{4,2},{6,0},{8,14},{10,12},{12,10},{14,8},{1,7},{3,5},... | collective-permute-start | bytes 196616 | tf_op jit(solution)/shard_map/projections/ppermute | solution.py:40
  165.8 2.9 %collective-permute-start.22 = (bf16[192,256]{1,0:T(8,128)(2,1)S(1)}, bf16[192,256]{1,0:T(8,128)(2,1)S(1)}, u32[]{:S(2)}, u32[]{:S(2)}) collective-permute-start(bf16[192,256]{1,0:T(8,128)(2,1)S(1)} %attend.1), channel_id=1, source_target_pairs={{0,8},{2,10},{4,12},{6,14},{8,0},{10,2},{12,4},{14,6},{1,9},{3,11}... | collective-permute-start | bytes 294920 | tf_op jit(solution)/shard_map/attention/ppermute | solution.py:40
  168.7 13.0 %collective-permute-done.22 = bf16[192,256]{1,0:T(8,128)(2,1)S(1)} collective-permute-done((bf16[192,256]{1,0:T(8,128)(2,1)S(1)}, bf16[192,256]{1,0:T(8,128)(2,1)S(1)}, u32[]{:S(2)}, u32[]{:S(2)}) %collective-permute-start.22) | collective-permute-done | bytes 98336 | tf_op jit(solution)/shard_map/attention/ppermute | solution.py:40
  185.5 5.4 %collective-permute-start.25 = (bf16[2,192,256]{2,1,0:T(8,128)(2,1)S(1)}, bf16[2,192,256]{2,1,0:T(8,128)(2,1)S(1)}, u32[]{:S(2)}, u32[]{:S(2)}) collective-permute-start(bf16[2,192,256]{2,1,0:T(8,128)(2,1)S(1)} %pad_maximum_fusion.3.refs_1_), channel_id=1, source_target_pairs={{0,6},{2,4},{4,2},{6,0},{8,14},{10,12},{12,10},{14,8},{1,7},{3,5},... | collective-permute-start | bytes 589832 | tf_op jit(solution)/shard_map/attention/ppermute | solution.py:40
  191.0 3.6 %all-gather.4.cloned.1.call-done = bf16[16,2,8,8,1024]{4,3,2,1,0:T(8,128)(2,1)} async-done(((bf16[1,2,8,8,1024]{4,3,2,1,0:T(8,128)(2,1)}), bf16[16,2,8,8,1024]{4,3,2,1,0:T(8,128)(2,1)}) %all-gather.4.cloned.1.call-update) | async-done | bytes 4194320 | tf_op jit(solution)/shard_map/out_weight/all_gather | solution.py:401
  194.6 2.6 %copy.28 = bf16[8,4,2,4,8,1024]{5,4,3,2,1,0:T(8,128)(2,1)S(1)} copy(bf16[8,4,2,4,8,1024]{5,4,0,2,3,1:T(8,128)(2,1)} %bitcast.41) | data formatting | bytes 8388608 | tf_op jit(solution)/shard_map/out_weight/transpose | solution.py:402
  197.2 3.3 %collective-permute-done.24.refs_3_ = bf16[2,192,256]{2,1,0:T(8,128)(2,1)S(1)} collective-permute-done((bf16[2,192,256]{2,1,0:T(8,128)(2,1)S(1)}, bf16[2,192,256]{2,1,0:T(8,128)(2,1)S(1)}, u32[]{:S(2)}, u32[]{:S(2)}) %collective-permute-start.24) | collective-permute-done | bytes 196640 | tf_op jit(solution)/shard_map/attention/ppermute | solution.py:40
  201.7 2.5 %collective-permute-start.26 = (bf16[192,512]{1,0:T(8,128)(2,1)S(1)}, bf16[192,512]{1,0:T(8,128)(2,1)S(1)}, u32[]{:S(2)}, u32[]{:S(2)}) collective-permute-start(bf16[192,512]{1,0:T(8,128)(2,1)S(1)} %output_other.1), channel_id=1, source_target_pairs={{0,1},{1,0},{2,3},{3,2},{4,5},{5,4},{6,7},{7,6},{8,9},{9,8},{10,11... | collective-permute-start | bytes 589832 | tf_op jit(solution)/shard_map/output/ppermute | solution.py:44
  (72 shorter events, 46.9 us)
Async XLA Ops:
  7.2 124.0 %all-gather.6.cloned.1.call-start = ((), (), s32[]{:S(2)}) async-start(), calls=%async_computation.1 | async-start | bytes 2228224 | tf_op jit(solution)/shard_map/out_columns/all_gather | solution.py:394
  9.5 36.2 %collective-permute-start.2 = (bf16[256,256]{1,0:T(8,128)(2,1)S(1)}, bf16[256,256]{1,0:T(8,128)(2,1)S(1)}, u32[]{:S(2)}, u32[]{:S(2)}) collective-permute-start(bf16[256,256]{1,0:T(8,128)(2,1)S(1)} %get-tuple-element.44), channel_id=1, source_target_pairs={{0,0},{1,1},{2,2},{3,3},{4,4},{5,5},{6,6},{7,7},{8,256},{9,257},{1... | collective-permute-start | bytes 393224 | tf_op jit(solution)/shard_map/in_weight/ppermute | solution.py:67
  10.3 36.7 %collective-permute-start.4 = (bf16[256,256]{1,0:T(8,128)(2,1)S(1)}, bf16[256,256]{1,0:T(8,128)(2,1)S(1)}, u32[]{:S(2)}, u32[]{:S(2)}) collective-permute-start(bf16[256,256]{1,0:T(8,128)(2,1)S(1)} %get-tuple-element.44), channel_id=1, source_target_pairs={{0,64},{1,65},{2,66},{3,67},{4,68},{5,69},{6,70},{7,71},{8,320},{9... | collective-permute-start | bytes 393224 | tf_op jit(solution)/shard_map/in_weight/ppermute | solution.py:67
  28.2 17.5 %collective-permute-start.3 = (bf16[64,256]{1,0:T(8,128)(2,1)S(1)}, bf16[64,256]{1,0:T(8,128)(2,1)S(1)}, u32[]{:S(2)}, u32[]{:S(2)}) collective-permute-start(bf16[64,256]{1,0:T(8,128)(2,1)S(1)} %bitcast.51), channel_id=1, source_target_pairs={{0,0},{1,256},{2,2},{3,258},{4,4},{5,260},{6,6},{7,262},{8,1},{9,2... | collective-permute-start | bytes 98312 | tf_op jit(solution)/shard_map/in_weight/ppermute | solution.py:67
  37.9 9.1 %collective-permute-start.5 = (bf16[64,256]{1,0:T(8,128)(2,1)S(1)}, bf16[64,256]{1,0:T(8,128)(2,1)S(1)}, u32[]{:S(2)}, u32[]{:S(2)}) collective-permute-start(bf16[64,256]{1,0:T(8,128)(2,1)S(1)} %bitcast.52), channel_id=1, source_target_pairs={{0,64},{1,320},{2,66},{3,322},{4,68},{5,324},{6,70},{7,326},{8,65}... | collective-permute-start | bytes 98312 | tf_op jit(solution)/shard_map/in_weight/ppermute | solution.py:67
  47.1 147.5 %all-gather.4.cloned.1.call-start = ((), (), s32[]{:S(2)}) async-start(), calls=%async_computation | async-start | bytes 4456448 | tf_op jit(solution)/shard_map/out_weight/all_gather | solution.py:401
  56.7 28.5 %collective-permute-start.6 = (bf16[2,192,256]{2,1,0:T(8,128)(2,1)S(1)}, bf16[2,192,256]{2,1,0:T(8,128)(2,1)S(1)}, u32[]{:S(2)}, u32[]{:S(2)}) collective-permute-start(bf16[2,192,256]{2,1,0:T(8,128)(2,1)S(1)} %pad_maximum_fusion.2.own), channel_id=1, source_target_pairs={{0,4},{2,6},{4,0},{6,2},{8,12},{10,14},{12,8},{14,10},{1,5},{3,7},... | collective-permute-start | bytes 589832 | tf_op jit(solution)/shard_map/tokens/ppermute | solution.py:40
  59.9 40.8 %collective-permute-start.10 = (bf16[2,320,256]{2,1,0:T(8,128)(2,1)S(1)}, bf16[2,320,256]{2,1,0:T(8,128)(2,1)S(1)}, u32[]{:S(2)}, u32[]{:S(2)}) collective-permute-start(bf16[2,320,256]{2,1,0:T(8,128)(2,1)S(1)} %pad_maximum_fusion.1.w0), channel_id=1, source_target_pairs={{0,128},{128,0},{256,384},{384,256},{1,129},{129,1},{257,385},{385... | collective-permute-start | bytes 983048 | tf_op jit(solution)/shard_map/tokens/ppermute | solution.py:52
  62.9 37.9 %collective-permute-start.11 = (bf16[2,320,256]{2,1,0:T(8,128)(2,1)S(1)}, bf16[2,320,256]{2,1,0:T(8,128)(2,1)S(1)}, u32[]{:S(2)}, u32[]{:S(2)}) collective-permute-start(bf16[2,320,256]{2,1,0:T(8,128)(2,1)S(1)} %pad_maximum_fusion.1.w0), channel_id=1, source_target_pairs={{0,256},{128,384},{256,0},{384,128},{1,257},{129,385},{257,1},{385... | collective-permute-start | bytes 983048 | tf_op jit(solution)/shard_map/tokens/ppermute | solution.py:52
  81.4 19.4 %collective-permute-start.12 = (bf16[2,320,256]{2,1,0:T(8,128)(2,1)S(1)}, bf16[2,320,256]{2,1,0:T(8,128)(2,1)S(1)}, u32[]{:S(2)}, u32[]{:S(2)}) collective-permute-start(bf16[2,320,256]{2,1,0:T(8,128)(2,1)S(1)} %pad_maximum_fusion.1.w0), channel_id=1, source_target_pairs={{0,384},{128,256},{256,128},{384,0},{1,385},{129,257},{257,129},{3... | collective-permute-start | bytes 983048 | tf_op jit(solution)/shard_map/tokens/ppermute | solution.py:52
  83.3 9.0 %collective-permute-start.7 = (bf16[2,192,256]{2,1,0:T(8,128)(2,1)S(1)}, bf16[2,192,256]{2,1,0:T(8,128)(2,1)S(1)}, u32[]{:S(2)}, u32[]{:S(2)}) collective-permute-start(bf16[2,192,256]{2,1,0:T(8,128)(2,1)S(1)} %pad_maximum_fusion.2.own), channel_id=1, source_target_pairs={{0,2},{2,0},{4,6},{6,4},{8,10},{10,8},{12,14},{14,12},{1,3},{3,1},... | collective-permute-start | bytes 589832 | tf_op jit(solution)/shard_map/tokens/ppermute | solution.py:40
  85.3 15.4 %collective-permute-start.8 = (bf16[2,192,256]{2,1,0:T(8,128)(2,1)S(1)}, bf16[2,192,256]{2,1,0:T(8,128)(2,1)S(1)}, u32[]{:S(2)}, u32[]{:S(2)}) collective-permute-start(bf16[2,192,256]{2,1,0:T(8,128)(2,1)S(1)} %pad_maximum_fusion.2.own), channel_id=1, source_target_pairs={{0,6},{2,4},{4,2},{6,0},{8,14},{10,12},{12,10},{14,8},{1,7},{3,5},... | collective-permute-start | bytes 589832 | tf_op jit(solution)/shard_map/tokens/ppermute | solution.py:40
  109.7 9.7 %collective-permute-start.14 = (bf16[528,256]{1,0:T(8,128)(2,1)S(1)}, bf16[528,256]{1,0:T(8,128)(2,1)S(1)}, u32[]{:S(2)}, u32[]{:S(2)}) collective-permute-start(bf16[528,256]{1,0:T(8,128)(2,1)S(1)} %get-tuple-element.30), channel_id=1, source_target_pairs={{0,16},{16,0},{32,48},{48,32},{1,17},{17,1},{33,49},{49,33},{2,18}... | collective-permute-start | bytes 811016 | tf_op jit(solution)/shard_map/projections/ppermute | solution.py:52
  112.5 11.3 %collective-permute-start.15 = (bf16[528,256]{1,0:T(8,128)(2,1)S(1)}, bf16[528,256]{1,0:T(8,128)(2,1)S(1)}, u32[]{:S(2)}, u32[]{:S(2)}) collective-permute-start(bf16[528,256]{1,0:T(8,128)(2,1)S(1)} %get-tuple-element.31), channel_id=1, source_target_pairs={{0,32},{16,48},{32,0},{48,16},{1,33},{17,49},{33,1},{49,17},{2,34}... | collective-permute-start | bytes 811016 | tf_op jit(solution)/shard_map/projections/ppermute | solution.py:52
  114.5 16.0 %collective-permute-start.16 = (bf16[528,256]{1,0:T(8,128)(2,1)S(1)}, bf16[528,256]{1,0:T(8,128)(2,1)S(1)}, u32[]{:S(2)}, u32[]{:S(2)}) collective-permute-start(bf16[528,256]{1,0:T(8,128)(2,1)S(1)} %get-tuple-element.32), channel_id=1, source_target_pairs={{0,48},{16,32},{32,16},{48,0},{1,49},{17,33},{33,17},{49,1},{2,50}... | collective-permute-start | bytes 811016 | tf_op jit(solution)/shard_map/projections/ppermute | solution.py:52
  132.9 13.6 %collective-permute-start.17 = (bf16[128,256]{1,0:T(8,128)(2,1)S(1)}, bf16[128,256]{1,0:T(8,128)(2,1)S(1)}, u32[]{:S(2)}, u32[]{:S(2)}) collective-permute-start(bf16[128,256]{1,0:T(8,128)(2,1)S(1)} %get-tuple-element.36), channel_id=1, source_target_pairs={{0,8},{2,10},{4,12},{6,14},{8,0},{10,2},{12,4},{14,6},{1,9},{3,11}... | collective-permute-start | bytes 196616 | tf_op jit(solution)/shard_map/projections/ppermute | solution.py:40
  146.6 17.9 %collective-permute-start.18 = (bf16[208,256]{1,0:T(8,128)(2,1)S(1)}, bf16[208,256]{1,0:T(8,128)(2,1)S(1)}, u32[]{:S(2)}, u32[]{:S(2)}) collective-permute-start(bf16[208,256]{1,0:T(8,128)(2,1)S(1)} %get-tuple-element.37), channel_id=1, source_target_pairs={{0,8},{2,10},{4,12},{6,14},{8,0},{10,2},{12,4},{14,6},{1,9},{3,11}... | collective-permute-start | bytes 319496 | tf_op jit(solution)/shard_map/projections/ppermute | solution.py:40
  148.5 13.9 %collective-permute-start.19 = (bf16[128,256]{1,0:T(8,128)(2,1)S(1)}, bf16[128,256]{1,0:T(8,128)(2,1)S(1)}, u32[]{:S(2)}, u32[]{:S(2)}) collective-permute-start(bf16[128,256]{1,0:T(8,128)(2,1)S(1)} %add_convert_fusion.1.p0), channel_id=1, source_target_pairs={{0,4},{2,6},{4,0},{6,2},{8,12},{10,14},{12,8},{14,10},{1,5},{3,7},... | collective-permute-start | bytes 196616 | tf_op jit(solution)/shard_map/projections/ppermute | solution.py:40
  154.9 8.2 %collective-permute-start.20 = (bf16[128,256]{1,0:T(8,128)(2,1)S(1)}, bf16[128,256]{1,0:T(8,128)(2,1)S(1)}, u32[]{:S(2)}, u32[]{:S(2)}) collective-permute-start(bf16[128,256]{1,0:T(8,128)(2,1)S(1)} %add_convert_fusion.1.p0), channel_id=1, source_target_pairs={{0,2},{2,0},{4,6},{6,4},{8,10},{10,8},{12,14},{14,12},{1,3},{3,1},... | collective-permute-start | bytes 196616 | tf_op jit(solution)/shard_map/projections/ppermute | solution.py:40
  156.9 7.6 %collective-permute-start.21 = (bf16[128,256]{1,0:T(8,128)(2,1)S(1)}, bf16[128,256]{1,0:T(8,128)(2,1)S(1)}, u32[]{:S(2)}, u32[]{:S(2)}) collective-permute-start(bf16[128,256]{1,0:T(8,128)(2,1)S(1)} %add_convert_fusion.1.p0), channel_id=1, source_target_pairs={{0,6},{2,4},{4,2},{6,0},{8,14},{10,12},{12,10},{14,8},{1,7},{3,5},... | collective-permute-start | bytes 196616 | tf_op jit(solution)/shard_map/projections/ppermute | solution.py:40
  165.8 15.9 %collective-permute-start.22 = (bf16[192,256]{1,0:T(8,128)(2,1)S(1)}, bf16[192,256]{1,0:T(8,128)(2,1)S(1)}, u32[]{:S(2)}, u32[]{:S(2)}) collective-permute-start(bf16[192,256]{1,0:T(8,128)(2,1)S(1)} %attend.1), channel_id=1, source_target_pairs={{0,8},{2,10},{4,12},{6,14},{8,0},{10,2},{12,4},{14,6},{1,9},{3,11}... | collective-permute-start | bytes 294920 | tf_op jit(solution)/shard_map/attention/ppermute | solution.py:40
  181.7 15.5 %collective-permute-start.23 = (bf16[2,192,256]{2,1,0:T(8,128)(2,1)S(1)}, bf16[2,192,256]{2,1,0:T(8,128)(2,1)S(1)}, u32[]{:S(2)}, u32[]{:S(2)}) collective-permute-start(bf16[2,192,256]{2,1,0:T(8,128)(2,1)S(1)} %pad_maximum_fusion.3.refs_1_), channel_id=1, source_target_pairs={{0,4},{2,6},{4,0},{6,2},{8,12},{10,14},{12,8},{14,10},{1,5},{3,7},... | collective-permute-start | bytes 589832 | tf_op jit(solution)/shard_map/attention/ppermute | solution.py:40
  183.6 16.9 %collective-permute-start.24 = (bf16[2,192,256]{2,1,0:T(8,128)(2,1)S(1)}, bf16[2,192,256]{2,1,0:T(8,128)(2,1)S(1)}, u32[]{:S(2)}, u32[]{:S(2)}) collective-permute-start(bf16[2,192,256]{2,1,0:T(8,128)(2,1)S(1)} %pad_maximum_fusion.3.refs_1_), channel_id=1, source_target_pairs={{0,2},{2,0},{4,6},{6,4},{8,10},{10,8},{12,14},{14,12},{1,3},{3,1},... | collective-permute-start | bytes 589832 | tf_op jit(solution)/shard_map/attention/ppermute | solution.py:40
  185.5 15.0 %collective-permute-start.25 = (bf16[2,192,256]{2,1,0:T(8,128)(2,1)S(1)}, bf16[2,192,256]{2,1,0:T(8,128)(2,1)S(1)}, u32[]{:S(2)}, u32[]{:S(2)}) collective-permute-start(bf16[2,192,256]{2,1,0:T(8,128)(2,1)S(1)} %pad_maximum_fusion.3.refs_1_), channel_id=1, source_target_pairs={{0,6},{2,4},{4,2},{6,0},{8,14},{10,12},{12,10},{14,8},{1,7},{3,5},... | collective-permute-start | bytes 589832 | tf_op jit(solution)/shard_map/attention/ppermute | solution.py:40
  (12 other events, 332.3 us)
Sparse Core Ops, SparseCore 0:
  47.2 73.9 all-gather.5
  133.1 61.4 all-gather.3

commit v4 on v3

--- a/solution.py
+++ b/solution.py
@@ -239,16 +239,21 @@
 
 
 def attend_kernel(
-    place, lengths, query, sums, got, p0, p2, p1, p3, out, held
+    place, lengths, query, sums, got, p0, p2, p1, p3, out, held, held_values
 ):
     z = place[0]
     squares = sums[...] + join_sum(got[Q_ROWS : Q_ROWS + SUM_ROWS, :])
     scale = lax.rsqrt(squares * (1.0 / 8192) + norm_eps)[0:1, :]
     for step, pair in ((0, p0), (2, p2), (1, p1), (3, p3)):
+        chip = (z & 3) ^ step
+        parts = []
         for at in range(2):
-            piece = pair[at * KV_ROWS : (at + 1) * KV_ROWS, :]
-            piece = piece.astype(jnp.float32) * scale
-            held[((z & 3) ^ step) * 2 + at] = piece.astype(jnp.bfloat16)
+            part = pair[at * KV_ROWS : (at + 1) * KV_ROWS, :]
+            part = part.astype(jnp.float32) * scale
+            held[chip * 2 + at] = part[0:32].astype(jnp.bfloat16)
+            parts.append(part[32:64])
+        rows = [part[n : n + 8] for n in range(0, 32, 8) for part in parts]
+        held_values[chip] = jnp.concatenate(rows).astype(jnp.bfloat16)
     column = jnp.broadcast_to(scale, (128, LANES)).T[0:ROWS, 0:1]
     heads = query[...] + got[0:Q_ROWS, :].astype(jnp.float32)
     heads = (heads * column).astype(jnp.bfloat16)
@@ -263,8 +268,8 @@
         key_doc = key_doc + (key_at >= end).astype(jnp.int32)
     allowed = (query_doc == key_doc) & (key_at <= query_at)
     for head in range(2):
-        keys = held[head * 4 : head * 4 + 4, 0:32, :].reshape(HEAD_DIM, LANES)
-        values = held[head * 4 : head * 4 + 4, 32:64, :].reshape(HEAD_DIM, LANES)
+        keys = held[head * 4 : head * 4 + 4].reshape(HEAD_DIM, LANES)
+        values = held_values[head * 2 : head * 2 + 2].reshape(HEAD_DIM, LANES)
         columns = slice(head * HEAD_DIM, (head + 1) * HEAD_DIM)
         scores = jnp.dot(heads[:, columns], keys, preferred_element_type=jnp.float32)
         scores = jnp.where(allowed, scores * HEAD_DIM**-0.5, -1e30)
@@ -286,7 +291,10 @@
         out_shape=jax.ShapeDtypeStruct((ROWS, 256), jnp.bfloat16),
         in_specs=[smem(), smem()] + vmem(7),
         out_specs=vmem(1)[0],
-        scratch_shapes=[pltpu.VMEM((8, KV_ROWS, LANES), jnp.bfloat16)],
+        scratch_shapes=[
+            pltpu.VMEM((8, 32, LANES), jnp.bfloat16),
+            pltpu.VMEM((4, 64, LANES), jnp.bfloat16),
+        ],
         compiler_params=params(8),
         cost_estimate=pl.CostEstimate(
             flops=8 * ROWS * ROWS * HEAD_DIM,
@@ -304,7 +312,7 @@
         part = (p0, p2, p1, p3)[at // 2][at % 2]
         total = total + jnp.dot(
             part,
-            weight[place[0] ^ ORDER[at], :, pl.ds(start, 512)],
+            weight[:, place[0] ^ ORDER[at], :, pl.ds(start, 512)].reshape(256, 512),
             preferred_element_type=jnp.float32,
         )
     out[...] = total.astype(out.dtype)
@@ -321,7 +329,7 @@
         ),
         in_specs=[smem()] + vmem(5),
         out_specs=vmem(1)[0],
-        compiler_params=params(24),
+        compiler_params=params(56),
         cost_estimate=pl.CostEstimate(
             flops=2 * ROWS * 2048 * 512, bytes_accessed=5 * MIB, transcendentals=0
         ),
@@ -395,12 +403,11 @@
         start = lax.axis_index("z") * 1024
         o_rows = after(o_rows, query)
         o_halves = lax.dynamic_slice_in_dim(o_rows, start, 1024, axis=2)
-        o_halves = o_halves.reshape(2, 8, 8, 1024)
+        o_halves = o_halves.reshape(2, 8, 8, 1024).transpose(1, 0, 2, 3)
+        o_halves = o_halves.reshape(8, 16, 1024)
 
     with jax.named_scope("out_weight"):
         o_whole = lax.all_gather(o_halves, ("x", "y"), axis=0, tiled=False)
-        o_whole = o_whole.reshape(4, 4, 2, 8, 8, 1024).transpose(3, 0, 2, 1, 4, 5)
-        o_whole = o_whole.reshape(8, 256, 1024)
 
     with jax.named_scope("attention"):
         context = attend(place, doc_lengths, query, sums, got, pieces)

time: 214 us -> 224 us (1.047)
  waiting for transfers between devices: 57.8 us -> 70.3 us
  starting transfers between devices: 123 us -> 115 us
  Pallas kernels: 7.84 us -> 13.3 us
    ppermute x4, waiting for transfers between devices: 1.32 us -> 10.9 us  [move_weight(): return lax.ppermute(value, ('x', 'h', 'y', 'z', 'c'), moves)]
    ppermute x4, starting transfers between devices: 33.5 us -> 24.2 us  [move_weight(): return lax.ppermute(value, ('x', 'h', 'y', 'z', 'c'), moves)]
    pallas_call x2, Pallas kernels: 2.29 us -> 7.78 us  [project_output(): pl.pallas_call(kernel, out_shape=jax.ShapeDtypeStruct((ROWS, 512), jnp.bf...]
    ppermute x12, waiting for transfers between devices: 38.4 us -> 43.3 us  [swap_z(): return lax.ppermute(value, 'z', [(z, z ^ bit) for z in range(8)])]
    all_gather x1, waiting for transfers between devices: 3.59 us -> 0.02 us  [shards(): o_whole = lax.all_gather(o_halves, ('x', 'y'), axis=0, tiled=False)]
  transfers between devices with their start and end apart: 29 -> 29, of which waited for: 15 -> 14; matrix products, arithmetic and copies ran while one was open for 3% -> 2% of each run, Pallas kernels for 3% -> 4%
where the time goes in v4:
time: 224 us; the launch traced here: 223 us
  starting transfers between devices  115 us (51%)
  waiting for transfers between devices  70.3 us (31%)
  between operations  14.6 us (7%)
  Pallas kernels  13.3 us (6%)
  other arithmetic  6.78 us (3%)
  local copies, waits for them, and re-layouts  2.56 us (1%)
    ppermute x12, waiting for transfers between devices, swap_z(): return lax.ppermute(value, 'z', [(z, z ^ bit) for z in range(8)])  43.3 us
    ppermute x12, starting transfers between devices, swap_z(): return lax.ppermute(value, 'z', [(z, z ^ bit) for z in range(8)])  43.2 us
    ppermute x6, starting transfers between devices, swap_line(): return lax.ppermute(value, axis, [(at, at ^ bits) for at in range(4)])  32.2 us
    ppermute x4, starting transfers between devices, move_weight(): return lax.ppermute(value, ('x', 'h', 'y', 'z', 'c'), moves)  24.2 us
    ppermute x6, waiting for transfers between devices, swap_line(): return lax.ppermute(value, axis, [(at, at ^ bits) for at in range(4)])  12.9 us
    ppermute x4, waiting for transfers between devices, move_weight(): return lax.ppermute(value, ('x', 'h', 'y', 'z', 'c'), moves)  10.9 us
    ppermute x2, starting transfers between devices, spread_groups(): got.append(lax.ppermute(piece, ('y', 'c'), moves))  8.15 us
    pallas_call x2, Pallas kernels, project_output(): pl.pallas_call(kernel, out_shape=jax.ShapeDtypeStruct((ROWS, 512), jnp.bf...  7.78 us
  transfers between devices with their start and end apart: 29, of which 14 were waited for; matrix products, arithmetic and copies ran while one was open for 2% of the time, Pallas kernels for 4%

profile of v4, /device:TPU:1, one launch (start us, length us, event | category | flops | bytes accessed | tf_op | source)
XLA Modules:
  0.0 222.8 jit_solution(11136916744448835084)
XLA Ops:
  8.9 19.3 %collective-permute-start.5 = (bf16[64,256]{1,0:T(8,128)(2,1)S(1)}, bf16[64,256]{1,0:T(8,128)(2,1)S(1)}, u32[]{:S(2)}, u32[]{:S(2)}) collective-permute-start(bf16[64,256]{1,0:T(8,128)(2,1)S(1)} %bitcast.50), channel_id=1, source_target_pairs={{0,64},{1,320},{2,66},{3,322},{4,68},{5,324},{6,70},{7,326},{8,65}... | collective-permute-start | bytes 98312 | tf_op jit(solution)/shard_map/in_weight/ppermute | solution.py:67
  36.4 10.9 %collective-permute-done.4 = bf16[256,256]{1,0:T(8,128)(2,1)S(1)} collective-permute-done((bf16[256,256]{1,0:T(8,128)(2,1)S(1)}, bf16[256,256]{1,0:T(8,128)(2,1)S(1)}, u32[]{:S(2)}, u32[]{:S(2)}) %collective-permute-start.4) | collective-permute-done | bytes 131104 | tf_op jit(solution)/shard_map/in_weight/ppermute | solution.py:67
  47.5 3.0 %collective-permute-start = (bf16[192,256]{1,0:T(8,128)(2,1)S(1)}, bf16[192,256]{1,0:T(8,128)(2,1)S(1)}, u32[]{:S(2)}, u32[]{:S(2)}) collective-permute-start(bf16[192,256]{1,0:T(8,128)(2,1)S(1)} %get-tuple-element.52), channel_id=1, source_target_pairs={{0,0},{1,32},{16,16},{17,48},{32,1},{33,33},{48,17},{49,49},{2,2},... | collective-permute-start | bytes 294920 | tf_op jit(solution)/shard_map/tokens/ppermute | solution.py:80
  50.5 5.1 %collective-permute-start.1 = (bf16[192,256]{1,0:T(8,128)(2,1)S(1)}, bf16[192,256]{1,0:T(8,128)(2,1)S(1)}, u32[]{:S(2)}, u32[]{:S(2)}) collective-permute-start(bf16[192,256]{1,0:T(8,128)(2,1)S(1)} %get-tuple-element.53), channel_id=1, source_target_pairs={{0,16},{1,48},{16,0},{17,32},{32,17},{33,49},{48,1},{49,33},{2,18}... | collective-permute-start | bytes 294920 | tf_op jit(solution)/shard_map/tokens/ppermute | solution.py:80
  58.0 3.7 %collective-permute-start.8 = (bf16[2,192,256]{2,1,0:T(8,128)(2,1)S(1)}, bf16[2,192,256]{2,1,0:T(8,128)(2,1)S(1)}, u32[]{:S(2)}, u32[]{:S(2)}) collective-permute-start(bf16[2,192,256]{2,1,0:T(8,128)(2,1)S(1)} %pad_maximum_fusion.2.own), channel_id=1, source_target_pairs={{0,6},{2,4},{4,2},{6,0},{8,14},{10,12},{12,10},{14,8},{1,7},{3,5},... | collective-permute-start | bytes 589832 | tf_op jit(solution)/shard_map/tokens/ppermute | solution.py:40
  61.7 18.1 %collective-permute-start.12 = (bf16[2,320,256]{2,1,0:T(8,128)(2,1)S(1)}, bf16[2,320,256]{2,1,0:T(8,128)(2,1)S(1)}, u32[]{:S(2)}, u32[]{:S(2)}) collective-permute-start(bf16[2,320,256]{2,1,0:T(8,128)(2,1)S(1)} %pad_maximum_fusion.1.w0), channel_id=1, source_target_pairs={{0,384},{128,256},{256,128},{384,0},{1,385},{129,257},{257,129},{3... | collective-permute-start | bytes 983048 | tf_op jit(solution)/shard_map/tokens/ppermute | solution.py:52
  86.1 5.4 %collective-permute-start.6 = (bf16[2,192,256]{2,1,0:T(8,128)(2,1)S(1)}, bf16[2,192,256]{2,1,0:T(8,128)(2,1)S(1)}, u32[]{:S(2)}, u32[]{:S(2)}) collective-permute-start(bf16[2,192,256]{2,1,0:T(8,128)(2,1)S(1)} %pad_maximum_fusion.2.own), channel_id=1, source_target_pairs={{0,4},{2,6},{4,0},{6,2},{8,12},{10,14},{12,8},{14,10},{1,5},{3,7},... | collective-permute-start | bytes 589832 | tf_op jit(solution)/shard_map/tokens/ppermute | solution.py:40
  91.6 4.2 %collective-permute-done.7 = bf16[2,192,256]{2,1,0:T(8,128)(2,1)S(1)} collective-permute-done((bf16[2,192,256]{2,1,0:T(8,128)(2,1)S(1)}, bf16[2,192,256]{2,1,0:T(8,128)(2,1)S(1)}, u32[]{:S(2)}, u32[]{:S(2)}) %collective-permute-start.7) | collective-permute-done | bytes 196640 | tf_op jit(solution)/shard_map/tokens/ppermute | solution.py:40
  95.8 5.5 %collective-permute-done.6 = bf16[2,192,256]{2,1,0:T(8,128)(2,1)S(1)} collective-permute-done((bf16[2,192,256]{2,1,0:T(8,128)(2,1)S(1)}, bf16[2,192,256]{2,1,0:T(8,128)(2,1)S(1)}, u32[]{:S(2)}, u32[]{:S(2)}) %collective-permute-start.6) | collective-permute-done | bytes 196640 | tf_op jit(solution)/shard_map/tokens/ppermute | solution.py:40
  110.4 3.5 %collective-permute-start.14 = (bf16[528,256]{1,0:T(8,128)(2,1)S(1)}, bf16[528,256]{1,0:T(8,128)(2,1)S(1)}, u32[]{:S(2)}, u32[]{:S(2)}) collective-permute-start(bf16[528,256]{1,0:T(8,128)(2,1)S(1)} %get-tuple-element.30), channel_id=1, source_target_pairs={{0,16},{16,0},{32,48},{48,32},{1,17},{17,1},{33,49},{49,33},{2,18}... | collective-permute-start | bytes 811016 | tf_op jit(solution)/shard_map/projections/ppermute | solution.py:52
  113.9 2.5 %collective-permute-start.15 = (bf16[528,256]{1,0:T(8,128)(2,1)S(1)}, bf16[528,256]{1,0:T(8,128)(2,1)S(1)}, u32[]{:S(2)}, u32[]{:S(2)}) collective-permute-start(bf16[528,256]{1,0:T(8,128)(2,1)S(1)} %get-tuple-element.31), channel_id=1, source_target_pairs={{0,32},{16,48},{32,0},{48,16},{1,33},{17,49},{33,1},{49,17},{2,34}... | collective-permute-start | bytes 811016 | tf_op jit(solution)/shard_map/projections/ppermute | solution.py:52
  116.4 3.7 %collective-permute-start.16 = (bf16[528,256]{1,0:T(8,128)(2,1)S(1)}, bf16[528,256]{1,0:T(8,128)(2,1)S(1)}, u32[]{:S(2)}, u32[]{:S(2)}) collective-permute-start(bf16[528,256]{1,0:T(8,128)(2,1)S(1)} %get-tuple-element.32), channel_id=1, source_target_pairs={{0,48},{16,32},{32,16},{48,0},{1,49},{17,33},{33,17},{49,1},{2,50}... | collective-permute-start | bytes 811016 | tf_op jit(solution)/shard_map/projections/ppermute | solution.py:52
  120.4 6.4 %collective-permute-done.15.p2 = bf16[528,256]{1,0:T(8,128)(2,1)S(1)} collective-permute-done((bf16[528,256]{1,0:T(8,128)(2,1)S(1)}, bf16[528,256]{1,0:T(8,128)(2,1)S(1)}, u32[]{:S(2)}, u32[]{:S(2)}) %collective-permute-start.15) | collective-permute-done | bytes 270368 | tf_op jit(solution)/shard_map/projections/ppermute | solution.py:52
  126.8 6.2 %collective-permute-done.16.p3 = bf16[528,256]{1,0:T(8,128)(2,1)S(1)} collective-permute-done((bf16[528,256]{1,0:T(8,128)(2,1)S(1)}, bf16[528,256]{1,0:T(8,128)(2,1)S(1)}, u32[]{:S(2)}, u32[]{:S(2)}) %collective-permute-start.16) | collective-permute-done | bytes 270368 | tf_op jit(solution)/shard_map/projections/ppermute | solution.py:52
  135.5 6.4 %collective-permute-start.17 = (bf16[128,256]{1,0:T(8,128)(2,1)S(1)}, bf16[128,256]{1,0:T(8,128)(2,1)S(1)}, u32[]{:S(2)}, u32[]{:S(2)}) collective-permute-start(bf16[128,256]{1,0:T(8,128)(2,1)S(1)} %get-tuple-element.36), channel_id=1, source_target_pairs={{0,8},{2,10},{4,12},{6,14},{8,0},{10,2},{12,4},{14,6},{1,9},{3,11}... | collective-permute-start | bytes 196616 | tf_op jit(solution)/shard_map/projections/ppermute | solution.py:40
  141.9 7.5 %collective-permute-done.17 = bf16[128,256]{1,0:T(8,128)(2,1)S(1)} collective-permute-done((bf16[128,256]{1,0:T(8,128)(2,1)S(1)}, bf16[128,256]{1,0:T(8,128)(2,1)S(1)}, u32[]{:S(2)}, u32[]{:S(2)}) %collective-permute-start.17) | collective-permute-done | bytes 65568 | tf_op jit(solution)/shard_map/projections/ppermute | solution.py:40
  151.3 6.6 %collective-permute-start.21 = (bf16[128,256]{1,0:T(8,128)(2,1)S(1)}, bf16[128,256]{1,0:T(8,128)(2,1)S(1)}, u32[]{:S(2)}, u32[]{:S(2)}) collective-permute-start(bf16[128,256]{1,0:T(8,128)(2,1)S(1)} %add_convert_fusion.1.p0), channel_id=1, source_target_pairs={{0,6},{2,4},{4,2},{6,0},{8,14},{10,12},{12,10},{14,8},{1,7},{3,5},... | collective-permute-start | bytes 196616 | tf_op jit(solution)/shard_map/projections/ppermute | solution.py:40
  167.6 3.8 %collective-permute-start.22 = (bf16[192,256]{1,0:T(8,128)(2,1)S(1)}, bf16[192,256]{1,0:T(8,128)(2,1)S(1)}, u32[]{:S(2)}, u32[]{:S(2)}) collective-permute-start(bf16[192,256]{1,0:T(8,128)(2,1)S(1)} %attend.1), channel_id=1, source_target_pairs={{0,8},{2,10},{4,12},{6,14},{8,0},{10,2},{12,4},{14,6},{1,9},{3,11}... | collective-permute-start | bytes 294920 | tf_op jit(solution)/shard_map/attention/ppermute | solution.py:40
  171.5 12.5 %collective-permute-done.22 = bf16[192,256]{1,0:T(8,128)(2,1)S(1)} collective-permute-done((bf16[192,256]{1,0:T(8,128)(2,1)S(1)}, bf16[192,256]{1,0:T(8,128)(2,1)S(1)}, u32[]{:S(2)}, u32[]{:S(2)}) %collective-permute-start.22) | collective-permute-done | bytes 98336 | tf_op jit(solution)/shard_map/attention/ppermute | solution.py:40
  187.9 5.4 %collective-permute-start.23 = (bf16[2,192,256]{2,1,0:T(8,128)(2,1)S(1)}, bf16[2,192,256]{2,1,0:T(8,128)(2,1)S(1)}, u32[]{:S(2)}, u32[]{:S(2)}) collective-permute-start(bf16[2,192,256]{2,1,0:T(8,128)(2,1)S(1)} %pad_maximum_fusion.3.refs_1_), channel_id=1, source_target_pairs={{0,4},{2,6},{4,0},{6,2},{8,12},{10,14},{12,8},{14,10},{1,5},{3,7},... | collective-permute-start | bytes 589832 | tf_op jit(solution)/shard_map/attention/ppermute | solution.py:40
  193.7 8.9 %collective-permute-done.24.refs_3_ = bf16[2,192,256]{2,1,0:T(8,128)(2,1)S(1)} collective-permute-done((bf16[2,192,256]{2,1,0:T(8,128)(2,1)S(1)}, bf16[2,192,256]{2,1,0:T(8,128)(2,1)S(1)}, u32[]{:S(2)}, u32[]{:S(2)}) %collective-permute-start.24) | collective-permute-done | bytes 196640 | tf_op jit(solution)/shard_map/attention/ppermute | solution.py:40
  203.4 3.9 %output_other.1 = bf16[192,512]{1,0:T(8,128)(2,1)} custom-call(s32[5]{0:T(128)} %copy-done.1, bf16[2,192,256]{2,1,0:T(8,128)(2,1)} %copy-done.3, bf16[2,192,256]{2,1,0:T(8,128)(2,1)} %copy-done.6, bf16[2,192,256]{2,1,0:T(8,128)(2,1)} %copy-done.5, bf16[2,192,256]{2,1,0:T(8,128)(2,1)} %copy-done.4, bf16[16,8,16,1024]{3,2,1,0:T(8,128)(2,1)} %all-gather.4.cloned.1.call-done.refs_5_), custom_call_target="tpu_custom_call" | custom-call | flops 402653184 | bytes 5242880 | tf_op jit(solution)/shard_map/output/output_other/pallas_call | solution.py:325
  207.2 3.1 %collective-permute-start.26 = (bf16[192,512]{1,0:T(8,128)(2,1)}, bf16[192,512]{1,0:T(8,128)(2,1)S(1)}, u32[]{:S(2)}, u32[]{:S(2)}) collective-permute-start(bf16[192,512]{1,0:T(8,128)(2,1)} %output_other.1), channel_id=1, source_target_pairs={{0,1},{1,0},{2,3},{3,2},{4,5},{5,4},{6,7},{7,6},{8,9},{9,8},{10,11... | collective-permute-start | bytes 589832 | tf_op jit(solution)/shard_map/output/ppermute | solution.py:44
  210.3 3.9 %output_own.1 = f32[192,512]{1,0:T(8,128)} custom-call(s32[5]{0:T(128)} %copy-done.1, bf16[2,192,256]{2,1,0:T(8,128)(2,1)} %copy-done.3, bf16[2,192,256]{2,1,0:T(8,128)(2,1)} %copy-done.6, bf16[2,192,256]{2,1,0:T(8,128)(2,1)} %copy-done.5, bf16[2,192,256]{2,1,0:T(8,128)(2,1)} %copy-done.4, bf16[16,8,16,1024]{3,2,1,0:T(8,128)(2,1)} %all-gather.4.cloned.1.call-done.refs_5_), custom_call_target="tpu_custom_call" | custom-call | flops 402653184 | bytes 5242880 | tf_op jit(solution)/shard_map/output/output_own/pallas_call | solution.py:325
  (82 shorter events, 48.7 us)
Async XLA Ops:
  7.2 126.5 %all-gather.6.cloned.1.call-start = ((), (), s32[]{:S(2)}) async-start(), calls=%async_computation.1 | async-start | bytes 2228224 | tf_op jit(solution)/shard_map/out_columns/all_gather | solution.py:402
  8.9 27.4 %collective-permute-start.5 = (bf16[64,256]{1,0:T(8,128)(2,1)S(1)}, bf16[64,256]{1,0:T(8,128)(2,1)S(1)}, u32[]{:S(2)}, u32[]{:S(2)}) collective-permute-start(bf16[64,256]{1,0:T(8,128)(2,1)S(1)} %bitcast.50), channel_id=1, source_target_pairs={{0,64},{1,320},{2,66},{3,322},{4,68},{5,324},{6,70},{7,326},{8,65}... | collective-permute-start | bytes 98312 | tf_op jit(solution)/shard_map/in_weight/ppermute | solution.py:67
  28.2 19.0 %collective-permute-start.3 = (bf16[64,256]{1,0:T(8,128)(2,1)S(1)}, bf16[64,256]{1,0:T(8,128)(2,1)S(1)}, u32[]{:S(2)}, u32[]{:S(2)}) collective-permute-start(bf16[64,256]{1,0:T(8,128)(2,1)S(1)} %bitcast.51), channel_id=1, source_target_pairs={{0,0},{1,256},{2,2},{3,258},{4,4},{5,260},{6,6},{7,262},{8,1},{9,2... | collective-permute-start | bytes 98312 | tf_op jit(solution)/shard_map/in_weight/ppermute | solution.py:67
  32.3 14.9 %collective-permute-start.4 = (bf16[256,256]{1,0:T(8,128)(2,1)S(1)}, bf16[256,256]{1,0:T(8,128)(2,1)S(1)}, u32[]{:S(2)}, u32[]{:S(2)}) collective-permute-start(bf16[256,256]{1,0:T(8,128)(2,1)S(1)} %get-tuple-element.44), channel_id=1, source_target_pairs={{0,64},{1,65},{2,66},{3,67},{4,68},{5,69},{6,70},{7,71},{8,320},{9... | collective-permute-start | bytes 393224 | tf_op jit(solution)/shard_map/in_weight/ppermute | solution.py:67
  34.6 12.6 %collective-permute-start.2 = (bf16[256,256]{1,0:T(8,128)(2,1)S(1)}, bf16[256,256]{1,0:T(8,128)(2,1)S(1)}, u32[]{:S(2)}, u32[]{:S(2)}) collective-permute-start(bf16[256,256]{1,0:T(8,128)(2,1)S(1)} %get-tuple-element.44), channel_id=1, source_target_pairs={{0,0},{1,1},{2,2},{3,3},{4,4},{5,5},{6,6},{7,7},{8,256},{9,257},{1... | collective-permute-start | bytes 393224 | tf_op jit(solution)/shard_map/in_weight/ppermute | solution.py:67
  47.4 155.3 %all-gather.4.cloned.1.call-start = ((), (), s32[]{:S(2)}) async-start(), calls=%async_computation | async-start | bytes 4456448 | tf_op jit(solution)/shard_map/out_weight/all_gather | solution.py:410
  47.5 8.2 %collective-permute-start = (bf16[192,256]{1,0:T(8,128)(2,1)S(1)}, bf16[192,256]{1,0:T(8,128)(2,1)S(1)}, u32[]{:S(2)}, u32[]{:S(2)}) collective-permute-start(bf16[192,256]{1,0:T(8,128)(2,1)S(1)} %get-tuple-element.52), channel_id=1, source_target_pairs={{0,0},{1,32},{16,16},{17,48},{32,1},{33,33},{48,17},{49,49},{2,2},... | collective-permute-start | bytes 294920 | tf_op jit(solution)/shard_map/tokens/ppermute | solution.py:80
  58.0 28.1 %collective-permute-start.8 = (bf16[2,192,256]{2,1,0:T(8,128)(2,1)S(1)}, bf16[2,192,256]{2,1,0:T(8,128)(2,1)S(1)}, u32[]{:S(2)}, u32[]{:S(2)}) collective-permute-start(bf16[2,192,256]{2,1,0:T(8,128)(2,1)S(1)} %pad_maximum_fusion.2.own), channel_id=1, source_target_pairs={{0,6},{2,4},{4,2},{6,0},{8,14},{10,12},{12,10},{14,8},{1,7},{3,5},... | collective-permute-start | bytes 589832 | tf_op jit(solution)/shard_map/tokens/ppermute | solution.py:40
  61.7 39.7 %collective-permute-start.12 = (bf16[2,320,256]{2,1,0:T(8,128)(2,1)S(1)}, bf16[2,320,256]{2,1,0:T(8,128)(2,1)S(1)}, u32[]{:S(2)}, u32[]{:S(2)}) collective-permute-start(bf16[2,320,256]{2,1,0:T(8,128)(2,1)S(1)} %pad_maximum_fusion.1.w0), channel_id=1, source_target_pairs={{0,384},{128,256},{256,128},{384,0},{1,385},{129,257},{257,129},{3... | collective-permute-start | bytes 983048 | tf_op jit(solution)/shard_map/tokens/ppermute | solution.py:52
  79.8 21.6 %collective-permute-start.11 = (bf16[2,320,256]{2,1,0:T(8,128)(2,1)S(1)}, bf16[2,320,256]{2,1,0:T(8,128)(2,1)S(1)}, u32[]{:S(2)}, u32[]{:S(2)}) collective-permute-start(bf16[2,320,256]{2,1,0:T(8,128)(2,1)S(1)} %pad_maximum_fusion.1.w0), channel_id=1, source_target_pairs={{0,256},{128,384},{256,0},{384,128},{1,257},{129,385},{257,1},{385... | collective-permute-start | bytes 983048 | tf_op jit(solution)/shard_map/tokens/ppermute | solution.py:52
  81.7 19.7 %collective-permute-start.10 = (bf16[2,320,256]{2,1,0:T(8,128)(2,1)S(1)}, bf16[2,320,256]{2,1,0:T(8,128)(2,1)S(1)}, u32[]{:S(2)}, u32[]{:S(2)}) collective-permute-start(bf16[2,320,256]{2,1,0:T(8,128)(2,1)S(1)} %pad_maximum_fusion.1.w0), channel_id=1, source_target_pairs={{0,128},{128,0},{256,384},{384,256},{1,129},{129,1},{257,385},{385... | collective-permute-start | bytes 983048 | tf_op jit(solution)/shard_map/tokens/ppermute | solution.py:52
  84.2 11.6 %collective-permute-start.7 = (bf16[2,192,256]{2,1,0:T(8,128)(2,1)S(1)}, bf16[2,192,256]{2,1,0:T(8,128)(2,1)S(1)}, u32[]{:S(2)}, u32[]{:S(2)}) collective-permute-start(bf16[2,192,256]{2,1,0:T(8,128)(2,1)S(1)} %pad_maximum_fusion.2.own), channel_id=1, source_target_pairs={{0,2},{2,0},{4,6},{6,4},{8,10},{10,8},{12,14},{14,12},{1,3},{3,1},... | collective-permute-start | bytes 589832 | tf_op jit(solution)/shard_map/tokens/ppermute | solution.py:40
  86.1 15.2 %collective-permute-start.6 = (bf16[2,192,256]{2,1,0:T(8,128)(2,1)S(1)}, bf16[2,192,256]{2,1,0:T(8,128)(2,1)S(1)}, u32[]{:S(2)}, u32[]{:S(2)}) collective-permute-start(bf16[2,192,256]{2,1,0:T(8,128)(2,1)S(1)} %pad_maximum_fusion.2.own), channel_id=1, source_target_pairs={{0,4},{2,6},{4,0},{6,2},{8,12},{10,14},{12,8},{14,10},{1,5},{3,7},... | collective-permute-start | bytes 589832 | tf_op jit(solution)/shard_map/tokens/ppermute | solution.py:40
  110.4 10.0 %collective-permute-start.14 = (bf16[528,256]{1,0:T(8,128)(2,1)S(1)}, bf16[528,256]{1,0:T(8,128)(2,1)S(1)}, u32[]{:S(2)}, u32[]{:S(2)}) collective-permute-start(bf16[528,256]{1,0:T(8,128)(2,1)S(1)} %get-tuple-element.30), channel_id=1, source_target_pairs={{0,16},{16,0},{32,48},{48,32},{1,17},{17,1},{33,49},{49,33},{2,18}... | collective-permute-start | bytes 811016 | tf_op jit(solution)/shard_map/projections/ppermute | solution.py:52
  113.9 12.9 %collective-permute-start.15 = (bf16[528,256]{1,0:T(8,128)(2,1)S(1)}, bf16[528,256]{1,0:T(8,128)(2,1)S(1)}, u32[]{:S(2)}, u32[]{:S(2)}) collective-permute-start(bf16[528,256]{1,0:T(8,128)(2,1)S(1)} %get-tuple-element.31), channel_id=1, source_target_pairs={{0,32},{16,48},{32,0},{48,16},{1,33},{17,49},{33,1},{49,17},{2,34}... | collective-permute-start | bytes 811016 | tf_op jit(solution)/shard_map/projections/ppermute | solution.py:52
  116.4 16.6 %collective-permute-start.16 = (bf16[528,256]{1,0:T(8,128)(2,1)S(1)}, bf16[528,256]{1,0:T(8,128)(2,1)S(1)}, u32[]{:S(2)}, u32[]{:S(2)}) collective-permute-start(bf16[528,256]{1,0:T(8,128)(2,1)S(1)} %get-tuple-element.32), channel_id=1, source_target_pairs={{0,48},{16,32},{32,16},{48,0},{1,49},{17,33},{33,17},{49,1},{2,50}... | collective-permute-start | bytes 811016 | tf_op jit(solution)/shard_map/projections/ppermute | solution.py:52
  135.5 13.9 %collective-permute-start.17 = (bf16[128,256]{1,0:T(8,128)(2,1)S(1)}, bf16[128,256]{1,0:T(8,128)(2,1)S(1)}, u32[]{:S(2)}, u32[]{:S(2)}) collective-permute-start(bf16[128,256]{1,0:T(8,128)(2,1)S(1)} %get-tuple-element.36), channel_id=1, source_target_pairs={{0,8},{2,10},{4,12},{6,14},{8,0},{10,2},{12,4},{14,6},{1,9},{3,11}... | collective-permute-start | bytes 196616 | tf_op jit(solution)/shard_map/projections/ppermute | solution.py:40
  149.3 17.0 %collective-permute-start.18 = (bf16[208,256]{1,0:T(8,128)(2,1)S(1)}, bf16[208,256]{1,0:T(8,128)(2,1)S(1)}, u32[]{:S(2)}, u32[]{:S(2)}) collective-permute-start(bf16[208,256]{1,0:T(8,128)(2,1)S(1)} %get-tuple-element.37), channel_id=1, source_target_pairs={{0,8},{2,10},{4,12},{6,14},{8,0},{10,2},{12,4},{14,6},{1,9},{3,11}... | collective-permute-start | bytes 319496 | tf_op jit(solution)/shard_map/projections/ppermute | solution.py:40
  151.3 12.7 %collective-permute-start.21 = (bf16[128,256]{1,0:T(8,128)(2,1)S(1)}, bf16[128,256]{1,0:T(8,128)(2,1)S(1)}, u32[]{:S(2)}, u32[]{:S(2)}) collective-permute-start(bf16[128,256]{1,0:T(8,128)(2,1)S(1)} %add_convert_fusion.1.p0), channel_id=1, source_target_pairs={{0,6},{2,4},{4,2},{6,0},{8,14},{10,12},{12,10},{14,8},{1,7},{3,5},... | collective-permute-start | bytes 196616 | tf_op jit(solution)/shard_map/projections/ppermute | solution.py:40
  157.9 8.5 %collective-permute-start.20 = (bf16[128,256]{1,0:T(8,128)(2,1)S(1)}, bf16[128,256]{1,0:T(8,128)(2,1)S(1)}, u32[]{:S(2)}, u32[]{:S(2)}) collective-permute-start(bf16[128,256]{1,0:T(8,128)(2,1)S(1)} %add_convert_fusion.1.p0), channel_id=1, source_target_pairs={{0,2},{2,0},{4,6},{6,4},{8,10},{10,8},{12,14},{14,12},{1,3},{3,1},... | collective-permute-start | bytes 196616 | tf_op jit(solution)/shard_map/projections/ppermute | solution.py:40
  167.6 16.3 %collective-permute-start.22 = (bf16[192,256]{1,0:T(8,128)(2,1)S(1)}, bf16[192,256]{1,0:T(8,128)(2,1)S(1)}, u32[]{:S(2)}, u32[]{:S(2)}) collective-permute-start(bf16[192,256]{1,0:T(8,128)(2,1)S(1)} %attend.1), channel_id=1, source_target_pairs={{0,8},{2,10},{4,12},{6,14},{8,0},{10,2},{12,4},{14,6},{1,9},{3,11}... | collective-permute-start | bytes 294920 | tf_op jit(solution)/shard_map/attention/ppermute | solution.py:40
  184.0 9.7 %collective-permute-start.25 = (bf16[2,192,256]{2,1,0:T(8,128)(2,1)S(1)}, bf16[2,192,256]{2,1,0:T(8,128)(2,1)S(1)}, u32[]{:S(2)}, u32[]{:S(2)}) collective-permute-start(bf16[2,192,256]{2,1,0:T(8,128)(2,1)S(1)} %pad_maximum_fusion.3.refs_1_), channel_id=1, source_target_pairs={{0,6},{2,4},{4,2},{6,0},{8,14},{10,12},{12,10},{14,8},{1,7},{3,5},... | collective-permute-start | bytes 589832 | tf_op jit(solution)/shard_map/attention/ppermute | solution.py:40
  185.9 16.7 %collective-permute-start.24 = (bf16[2,192,256]{2,1,0:T(8,128)(2,1)S(1)}, bf16[2,192,256]{2,1,0:T(8,128)(2,1)S(1)}, u32[]{:S(2)}, u32[]{:S(2)}) collective-permute-start(bf16[2,192,256]{2,1,0:T(8,128)(2,1)S(1)} %pad_maximum_fusion.3.refs_1_), channel_id=1, source_target_pairs={{0,2},{2,0},{4,6},{6,4},{8,10},{10,8},{12,14},{14,12},{1,3},{3,1},... | collective-permute-start | bytes 589832 | tf_op jit(solution)/shard_map/attention/ppermute | solution.py:40
  187.9 14.8 %collective-permute-start.23 = (bf16[2,192,256]{2,1,0:T(8,128)(2,1)S(1)}, bf16[2,192,256]{2,1,0:T(8,128)(2,1)S(1)}, u32[]{:S(2)}, u32[]{:S(2)}) collective-permute-start(bf16[2,192,256]{2,1,0:T(8,128)(2,1)S(1)} %pad_maximum_fusion.3.refs_1_), channel_id=1, source_target_pairs={{0,4},{2,6},{4,0},{6,2},{8,12},{10,14},{12,8},{14,10},{1,5},{3,7},... | collective-permute-start | bytes 589832 | tf_op jit(solution)/shard_map/attention/ppermute | solution.py:40
  (17 other events, 373.5 us)
Sparse Core Ops, SparseCore 0:
  47.5 76.2 all-gather.5
  135.6 62.2 all-gather.3
